TPU v7x, 128 devices: a whole 4x4x4 slice. The times are simulated.
128 devices in a mesh: col: 4 (over y_hi, core), row: 32 (over z, y_lo, x).
Axes of the slice: x: 4, y: 4 (y_hi: 2, y_lo: 2; y = y_hi * 2 + y_lo), z: 4, core: 2. Of those that a mesh axis runs over, the one named last changes fastest.
Arguments:
- panel: bfloat16 [32, 48, 512, 128], P('row', 'col'), may hold values from -6 to 6
- stiffness: bfloat16 [32, 48, 512, 512], P('row', 'col'), may hold values from -0.25 to 0.25
- mass: float32 [32, 48, 512], P('row', 'col'), may hold values from 0.2 to 2
- resident: bfloat16 [32, 24576, 1024], P('row', None, 'col'), may hold values from -0.013671875 to 0.013671875
- face_rows: int32 [32, 2, 2048], P('row'), may hold values from 0 to 24575, as said below
- counts: int32 [32], P('row'), may hold values from 24 to 48, as said below
Outputs:
- gram: float32 [1024, 128], P(('col', 'row'))
Inputs may be any that keep to these rules, and one draw needn't show every extreme that they name: `counts`: each partition has between 24 and 48 live elements in its first slots; some partition has exactly 48. `face_rows`: each list of a partition holds 2048 distinct node rows of its live elements; its list 0 includes its last live node row.
All inputs are finite; a program needn't handle non-finite values.
Results may differ from a plain program's by a relative error of at most 0.0034.
Values may be sent and summed in bfloat16 or wider, within the bound.
No kernel may reach another device: no remote copies, remote signals or barrier semaphores. Data moves between devices by JAX's collectives and lax.ppermute only.
A program may use at most 128 MiB of HBM per device.

v0:
```python
import jax
import jax.numpy as jnp
from jax import lax
from jax.sharding import PartitionSpec as P


def passed_along(value, axis, steps):
    count = lax.axis_size(axis)
    leading, last = (max(0, -steps), min(count, count - steps))
    return lax.ppermute(value, axis, [(source, source + steps) for source in range(leading, last)])


def shards(panel, stiffness, mass, resident, face_rows, counts):
    slots = panel.shape[1]
    nodes = panel.shape[2]
    width = panel.shape[3]
    column = lax.axis_index("col")
    slot_ids = column * slots + jnp.arange(slots, dtype=jnp.int32)
    live = slot_ids < counts[0]
    values = panel[0]
    applied = jnp.einsum("enm,ems->ens", stiffness[0], values, preferred_element_type=jnp.float32)
    applied = applied + mass[0][:, :, None] * values.astype(jnp.float32)
    applied = jnp.where(live[:, None, None], applied, 0.0).astype(jnp.bfloat16)
    local_rows = applied.reshape(slots * nodes, width)
    whole = lax.all_gather(local_rows, "col", axis=0, tiled=True)
    prev_rows = face_rows[0, 0]
    next_rows = face_rows[0, 1]
    from_next = passed_along(whole[prev_rows], "row", -1)
    from_prev = passed_along(whole[next_rows], "row", 1)
    summed = whole.astype(jnp.float32)
    summed = summed.at[next_rows].add(from_next.astype(jnp.float32))
    summed = summed.at[prev_rows].add(from_prev.astype(jnp.float32))
    summed = summed.astype(jnp.bfloat16)
    columns = resident[0]
    contract = (((0,), (0,)), ((), ()))
    own_rows = columns.shape[1] // lax.axis_size("row")
    partial_gram = lax.dot_general(columns, summed, contract, preferred_element_type=jnp.float32)
    full_gram = lax.psum(partial_gram, "row")
    gram = lax.dynamic_slice_in_dim(full_gram, lax.axis_index("row") * own_rows, own_rows, 0)
    return gram


def solution(mesh):
    in_specs = (
        P("row", "col", None, None),
        P("row", "col", None, None),
        P("row", "col", None),
        P("row", None, "col"),
        P("row", None, None),
        P("row"),
    )
    out_specs = P(("col", "row"), None)
    return jax.shard_map(shards, mesh=mesh, in_specs=in_specs, out_specs=out_specs, check_vma=False)
```

profile of v0, /device:TPU:0, one launch (start us, length us, event | category | flops | bytes accessed | tf_op | source)
XLA Modules:
  0.0 438.1 jit_solution(3387449314331696691)
XLA Ops:
  6.5 0.0 all-gather.2.cloned.1.call-start
  7.2 0.7 copy.11
  7.9 0.0 copy-start
  7.9 6.7 %select_convert_fusion = bf16[12,512,128]{2,1,0:T(8,128)(2,1)} fusion(bf16[1,12,512,512]{3,2,1,0:T(8,128)(2,1)} %param.7, bf16[1,12,512,128]{3,2,1,0:T(8,128)(2,1)} %param.6, f32[12,512]{1,0:T(8,128)S(1)} %bitcast.28, pred[12]{0:T(512)(128)(4,1)S(1)} %add_compare_fusion), kind=kOutput, calls=%fused_computation.9 | convolution fusion | flops 809238528 | bytes 9461772 | tf_op jit(solution)/shard_map/enm,ems->ens/dot_general | solution.py:21
  14.6 0.0 all-gather.2.cloned.1.call-update
  14.6 0.0 all-reduce.2.cloned.1.call-start
  14.7 0.0 copy-done
  14.7 52.9 %all-gather.2.cloned.1.call-done = bf16[24576,128]{1,0:T(8,128)(2,1)} async-done(((bf16[6144,128]{1,0:T(8,128)(2,1)}), bf16[24576,128]{1,0:T(8,128)(2,1)}) %all-gather.2.cloned.1.call-update) | async-done | bytes 6291472 | tf_op jit(solution)/shard_map/all_gather | solution.py:25
  67.7 9.2 %gather_fusion = bf16[2048,128]{1,0:T(8,128)(2,1)S(1)} fusion(bf16[24576,128]{1,0:T(8,128)(2,1)} %all-gather.2.cloned.1.call-done, s32[2048]{0:T(1024)S(1)} %broadcast_clamp_fusion.1), kind=kCustom, calls=%fused_computation | custom fusion | bytes 1056768 | tf_op jit(solution)/shard_map/gather | solution.py:28
  76.9 1.3 collective-permute-start
  78.2 9.2 %gather_fusion.1 = bf16[2048,128]{1,0:T(8,128)(2,1)S(1)} fusion(bf16[24576,128]{1,0:T(8,128)(2,1)} %all-gather.2.cloned.1.call-done, s32[2048]{0:T(1024)S(1)} %broadcast_clamp_fusion), kind=kCustom, calls=%fused_computation.1 | custom fusion | bytes 1056768 | tf_op jit(solution)/shard_map/gather | solution.py:29
  87.4 4.6 %collective-permute-start.1 = (bf16[2048,128]{1,0:T(8,128)(2,1)S(1)}, bf16[2048,128]{1,0:T(8,128)(2,1)S(1)}, u32[]{:S(2)}, u32[]{:S(2)}) collective-permute-start(bf16[2048,128]{1,0:T(8,128)(2,1)S(1)} %gather_fusion.1), channel_id=1, source_target_pairs={{0,1},{1,2},{2,3},{3,4},{4,5},{5,6},{6,7},{7,8},{8,9},{9,10},{10,1... | collective-permute-start | bytes 1572872 | tf_op jit(solution)/shard_map/ppermute | solution.py:10
  92.0 7.3 %convert_element_type.20 = f32[24576,128]{1,0:T(8,128)} convert(bf16[24576,128]{1,0:T(8,128)(2,1)} %all-gather.2.cloned.1.call-done) | non-fusion elementwise | flops 3145728 | bytes 18874368 | tf_op jit(solution)/shard_map/convert_element_type | solution.py:30
  99.3 0.0 collective-permute-done
  99.3 19.5 %scatter_custom_fusion = f32[24576,128]{1,0:T(8,128)} fusion(f32[24576,128]{1,0:T(8,128)} %convert_element_type.20, s32[2048]{0:T(1024)S(1)} %bitcast.32, bf16[2048,128]{1,0:T(8,128)(2,1)S(1)} %collective-permute-done), kind=kCustom, calls=%fused_computation.14 | custom fusion | flops 524288 | bytes 13107200 | tf_op jit(solution)/shard_map/scatter-add | solution.py:31
  118.8 0.0 collective-permute-done.1
  118.8 19.5 %scatter_custom_fusion.1 = f32[24576,128]{1,0:T(8,128)} fusion(f32[24576,128]{1,0:T(8,128)} %scatter_custom_fusion, s32[2048]{0:T(1024)S(1)} %bitcast.30, bf16[2048,128]{1,0:T(8,128)(2,1)S(1)} %collective-permute-done.1), kind=kCustom, calls=%fused_computation.12 | custom fusion | flops 524288 | bytes 13107200 | tf_op jit(solution)/shard_map/scatter-add | solution.py:32
  138.3 10.8 %fusion.8 = f32[256,128]{0,1:T(8,128)} fusion(bf16[1,24576,256]{2,1,0:T(8,128)(2,1)} %param.9, f32[24576,128]{1,0:T(8,128)} %scatter_custom_fusion.1), kind=kOutput, calls=%fused_computation.11 | convolution fusion | flops 1613758464 | bytes 25296896 | tf_op jit(solution)/shard_map/dot_general | solution.py:37
  149.1 0.0 all-reduce.2.cloned.1.call-update
  149.1 280.5 %all-reduce.2.cloned.1.call-done = f32[256,128]{0,1:T(8,128)} async-done(((f32[256,128]{0,1:T(8,128)}), f32[256,128]{0,1:T(8,128)}) %all-reduce.2.cloned.1.call-update) | async-done | bytes 131088 | tf_op jit(solution)/shard_map/psum | solution.py:38
  429.7 0.9 constant_dynamic-slice_fusion
  430.6 0.7 copy.8
  (4 shorter events, 0.0 us)
Async XLA Ops:
  6.5 61.1 %all-gather.2.cloned.1.call-start = ((), (), s32[]{:S(2)}) async-start(), calls=%async_computation | async-start | bytes 7864320 | tf_op jit(solution)/shard_map/all_gather | solution.py:25
  7.9 6.7 %copy-start = (s32[1,2,2048]{2,1,0:T(2,128)S(1)}, s32[1,2,2048]{2,1,0:T(2,128)}, u32[]{:S(2)}) copy-start(s32[1,2,2048]{2,1,0:T(2,128)} %param.10) | copy-start | bytes 49156
  14.6 415.0 %all-reduce.2.cloned.1.call-start = ((), (), s32[]{:S(2)}) async-start(), calls=%async_computation.1 | async-start | bytes 262144 | tf_op jit(solution)/shard_map/psum | solution.py:38
  76.9 22.4 %collective-permute-start = (bf16[2048,128]{1,0:T(8,128)(2,1)S(1)}, bf16[2048,128]{1,0:T(8,128)(2,1)S(1)}, u32[]{:S(2)}, u32[]{:S(2)}) collective-permute-start(bf16[2048,128]{1,0:T(8,128)(2,1)S(1)} %gather_fusion), channel_id=1, source_target_pairs={{1,0},{2,1},{3,2},{4,3},{5,4},{6,5},{7,6},{8,7},{9,8},{10,9},{11,1... | collective-permute-start | bytes 1572872 | tf_op jit(solution)/shard_map/ppermute | solution.py:10
  87.4 31.4 %collective-permute-start.1 = (bf16[2048,128]{1,0:T(8,128)(2,1)S(1)}, bf16[2048,128]{1,0:T(8,128)(2,1)S(1)}, u32[]{:S(2)}, u32[]{:S(2)}) collective-permute-start(bf16[2048,128]{1,0:T(8,128)(2,1)S(1)} %gather_fusion.1), channel_id=1, source_target_pairs={{0,1},{1,2},{2,3},{3,4},{4,5},{5,6},{6,7},{7,8},{8,9},{9,10},{10,1... | collective-permute-start | bytes 1572872 | tf_op jit(solution)/shard_map/ppermute | solution.py:10
Sparse Core Ops, SparseCore 0:
  14.7 52.8 all-gather.1
  149.3 280.3 all-reduce.1
where the time goes:
time: 439 us; the launch traced here: 438 us
  waiting for transfers between devices  333 us (76%)
  other arithmetic  46.4 us (11%)
  local copies, waits for them, and re-layouts  20.7 us (5%)
  matrix products  17.5 us (4%)
  between operations  14.1 us (3%)
  starting transfers between devices  5.91 us (1%)
    psum x1, waiting for transfers between devices, shards(): full_gram = lax.psum(partial_gram, 'row')  281 us
    all_gather x1, waiting for transfers between devices, shards(): whole = lax.all_gather(local_rows, 'col', axis=0, tiled=True)  52.9 us
    scatter-add x1, other arithmetic, shards(): summed = summed.at[prev_rows].add(from_prev.astype(jnp.float32))  19.5 us
    scatter-add x1, other arithmetic, shards(): summed = summed.at[next_rows].add(from_next.astype(jnp.float32))  19.5 us
    dot_general x1, matrix products, shards(): lax.dot_general(columns, summed, contract, preferred_element_type=jnp.flo...  10.8 us
    gather x1, local copies, waits for them, and re-layouts, shards(): from_prev = passed_along(whole[next_rows], 'row', 1)  9.19 us
    gather x1, local copies, waits for them, and re-layouts, shards(): from_next = passed_along(whole[prev_rows], 'row', -1)  9.19 us
  transfers between devices with their start and end apart: 4, of which 2 were waited for; matrix products, arithmetic and copies ran while one was open for 8% of the time, Pallas kernels for 0%

commit v1 on v0

--- a/solution.py
+++ b/solution.py
@@ -35,8 +35,9 @@
     contract = (((0,), (0,)), ((), ()))
     own_rows = columns.shape[1] // lax.axis_size("row")
     partial_gram = lax.dot_general(columns, summed, contract, preferred_element_type=jnp.float32)
-    full_gram = lax.psum(partial_gram, "row")
-    gram = lax.dynamic_slice_in_dim(full_gram, lax.axis_index("row") * own_rows, own_rows, 0)
+    tiles = partial_gram.reshape(lax.axis_size("row"), own_rows, width)
+    received = lax.all_to_all(tiles, "row", 0, 0)
+    gram = jnp.sum(received, axis=0)
     return gram
 
 

time: 439 us -> 175 us (0.40)
  waiting for transfers between devices: 333 us -> 53 us
  blocking collectives: 0 us -> 18.5 us
    psum x1 -> x0, waiting for transfers between devices: 281 us -> none  [shards(): full_gram = lax.psum(partial_gram, 'row')]
    all_to_all x0 -> x1, blocking collectives: none -> 18.5 us  [shards(): received = lax.all_to_all(tiles, 'row', 0, 0)]
  transfers between devices with their start and end apart: 4 -> 3, of which waited for: 2 -> 1; matrix products, arithmetic and copies ran while one was open for 8% -> 21% of each run, Pallas kernels for 0% -> 0%
where the time goes in v1:
time: 175 us
  waiting for transfers between devices  53 us (30%)
  other arithmetic  47 us (27%)
  local copies, waits for them, and re-layouts  19.2 us (11%)
  blocking collectives  18.5 us (11%)
  matrix products  16.8 us (10%)
  between operations  14.1 us (8%)
  starting transfers between devices  5.87 us (3%)
    all_gather x1, waiting for transfers between devices, shards(): whole = lax.all_gather(local_rows, 'col', axis=0, tiled=True)  53 us
    scatter-add x1, other arithmetic, shards(): summed = summed.at[next_rows].add(from_next.astype(jnp.float32))  19.5 us
    scatter-add x1, other arithmetic, shards(): summed = summed.at[prev_rows].add(from_prev.astype(jnp.float32))  19.5 us
    all_to_all x1, blocking collectives, shards(): received = lax.all_to_all(tiles, 'row', 0, 0)  18.5 us
    dot_general x1, matrix products, shards(): lax.dot_general(columns, summed, contract, preferred_element_type=jnp.flo...  10.2 us
    gather x1, local copies, waits for them, and re-layouts, shards(): from_prev = passed_along(whole[next_rows], 'row', 1)  9.19 us
    gather x1, local copies, waits for them, and re-layouts, shards(): from_next = passed_along(whole[prev_rows], 'row', -1)  9.19 us
    convert_element_type x1, other arithmetic, shards(): summed = whole.astype(jnp.float32)  7.36 us
  transfers between devices with their start and end apart: 3, of which 1 were waited for; matrix products, arithmetic and copies ran while one was open for 21% of the time, Pallas kernels for 0%

profile of v1, /device:TPU:0, one launch (start us, length us, event | category | flops | bytes accessed | tf_op | source)
XLA Modules:
  0.0 174.6 jit_solution(6502882506970696781)
XLA Ops:
  6.5 0.0 all-gather.2.cloned.1.call-start
  7.2 0.7 copy.10
  7.9 0.0 copy-start
  7.9 6.7 %select_convert_fusion = bf16[12,512,128]{2,1,0:T(8,128)(2,1)} fusion(bf16[1,12,512,512]{3,2,1,0:T(8,128)(2,1)} %param.7, bf16[1,12,512,128]{3,2,1,0:T(8,128)(2,1)} %param.6, f32[12,512]{1,0:T(8,128)S(1)} %bitcast.30, pred[12]{0:T(512)(128)(4,1)S(1)} %add_compare_fusion), kind=kOutput, calls=%fused_computation.9 | convolution fusion | flops 809238528 | bytes 9461772 | tf_op jit(solution)/shard_map/enm,ems->ens/dot_general | solution.py:21
  14.6 0.0 all-gather.2.cloned.1.call-update
  14.6 0.0 copy-done
  14.7 53.0 %all-gather.2.cloned.1.call-done = bf16[24576,128]{1,0:T(8,128)(2,1)} async-done(((bf16[6144,128]{1,0:T(8,128)(2,1)}), bf16[24576,128]{1,0:T(8,128)(2,1)}) %all-gather.2.cloned.1.call-update) | async-done | bytes 6291472 | tf_op jit(solution)/shard_map/all_gather | solution.py:25
  67.7 9.2 %gather_fusion = bf16[2048,128]{1,0:T(8,128)(2,1)S(1)} fusion(bf16[24576,128]{1,0:T(8,128)(2,1)} %all-gather.2.cloned.1.call-done, s32[2048]{0:T(1024)S(1)} %broadcast_clamp_fusion.1), kind=kCustom, calls=%fused_computation | custom fusion | bytes 1056768 | tf_op jit(solution)/shard_map/gather | solution.py:28
  76.9 1.3 collective-permute-start
  78.2 9.2 %gather_fusion.1 = bf16[2048,128]{1,0:T(8,128)(2,1)S(1)} fusion(bf16[24576,128]{1,0:T(8,128)(2,1)} %all-gather.2.cloned.1.call-done, s32[2048]{0:T(1024)S(1)} %broadcast_clamp_fusion), kind=kCustom, calls=%fused_computation.1 | custom fusion | bytes 1056768 | tf_op jit(solution)/shard_map/gather | solution.py:29
  87.4 4.6 %collective-permute-start.1 = (bf16[2048,128]{1,0:T(8,128)(2,1)S(1)}, bf16[2048,128]{1,0:T(8,128)(2,1)S(1)}, u32[]{:S(2)}, u32[]{:S(2)}) collective-permute-start(bf16[2048,128]{1,0:T(8,128)(2,1)S(1)} %gather_fusion.1), channel_id=1, source_target_pairs={{0,1},{1,2},{2,3},{3,4},{4,5},{5,6},{6,7},{7,8},{8,9},{9,10},{10,1... | collective-permute-start | bytes 1572872 | tf_op jit(solution)/shard_map/ppermute | solution.py:10
  91.9 7.4 %convert_element_type.20 = f32[24576,128]{1,0:T(8,128)} convert(bf16[24576,128]{1,0:T(8,128)(2,1)} %all-gather.2.cloned.1.call-done) | non-fusion elementwise | flops 3145728 | bytes 18874368 | tf_op jit(solution)/shard_map/convert_element_type | solution.py:30
  99.3 0.0 collective-permute-done
  99.3 19.5 %scatter_custom_fusion = f32[24576,128]{1,0:T(8,128)} fusion(f32[24576,128]{1,0:T(8,128)} %convert_element_type.20, s32[2048]{0:T(1024)S(1)} %bitcast.34, bf16[2048,128]{1,0:T(8,128)(2,1)S(1)} %collective-permute-done), kind=kCustom, calls=%fused_computation.14 | custom fusion | flops 524288 | bytes 13107200 | tf_op jit(solution)/shard_map/scatter-add | solution.py:31
  118.8 0.0 collective-permute-done.1
  118.8 19.5 %scatter_custom_fusion.1 = f32[24576,128]{1,0:T(8,128)} fusion(f32[24576,128]{1,0:T(8,128)} %scatter_custom_fusion, s32[2048]{0:T(1024)S(1)} %bitcast.32, bf16[2048,128]{1,0:T(8,128)(2,1)S(1)} %collective-permute-done.1), kind=kCustom, calls=%fused_computation.12 | custom fusion | flops 524288 | bytes 13107200 | tf_op jit(solution)/shard_map/scatter-add | solution.py:32
  138.3 10.2 %fusion.8 = f32[256,128]{0,1:T(8,128)S(1)} fusion(bf16[1,24576,256]{2,1,0:T(8,128)(2,1)} %param.9, f32[24576,128]{1,0:T(8,128)} %scatter_custom_fusion.1), kind=kOutput, calls=%fused_computation.11 | convolution fusion | flops 1613758464 | bytes 25296896 | tf_op jit(solution)/shard_map/dot_general | solution.py:37
  148.5 0.1 copy.7
  148.6 18.5 %all_to_all.5 = f32[32,8,128]{2,1,0:T(8,128)S(1)} all-to-all(f32[32,8,128]{2,1,0:T(8,128)S(1)} %bitcast.29), channel_id=1, replica_groups=mesh['col'=4,'row'=32] {'row'}, dimensions={0} | all-to-all | bytes 262144 | tf_op jit(solution)/shard_map/all_to_all | solution.py:39
  167.1 0.6 reduce_sum.9
  (4 shorter events, 0.0 us)
Async XLA Ops:
  6.5 61.1 %all-gather.2.cloned.1.call-start = ((), (), s32[]{:S(2)}) async-start(), calls=%async_computation.1 | async-start | bytes 7864320 | tf_op jit(solution)/shard_map/all_gather | solution.py:25
  7.9 6.7 %copy-start = (s32[1,2,2048]{2,1,0:T(2,128)S(1)}, s32[1,2,2048]{2,1,0:T(2,128)}, u32[]{:S(2)}) copy-start(s32[1,2,2048]{2,1,0:T(2,128)} %param.10) | copy-start | bytes 49156
  76.9 22.4 %collective-permute-start = (bf16[2048,128]{1,0:T(8,128)(2,1)S(1)}, bf16[2048,128]{1,0:T(8,128)(2,1)S(1)}, u32[]{:S(2)}, u32[]{:S(2)}) collective-permute-start(bf16[2048,128]{1,0:T(8,128)(2,1)S(1)} %gather_fusion), channel_id=1, source_target_pairs={{1,0},{2,1},{3,2},{4,3},{5,4},{6,5},{7,6},{8,7},{9,8},{10,9},{11,1... | collective-permute-start | bytes 1572872 | tf_op jit(solution)/shard_map/ppermute | solution.py:10
  87.4 31.4 %collective-permute-start.1 = (bf16[2048,128]{1,0:T(8,128)(2,1)S(1)}, bf16[2048,128]{1,0:T(8,128)(2,1)S(1)}, u32[]{:S(2)}, u32[]{:S(2)}) collective-permute-start(bf16[2048,128]{1,0:T(8,128)(2,1)S(1)} %gather_fusion.1), channel_id=1, source_target_pairs={{0,1},{1,2},{2,3},{3,4},{4,5},{5,6},{6,7},{7,8},{8,9},{9,10},{10,1... | collective-permute-start | bytes 1572872 | tf_op jit(solution)/shard_map/ppermute | solution.py:10
Sparse Core Ops, SparseCore 0:
  14.7 52.8 all-gather.1

commit v2 on v0

v2 whole, which is shorter than its diff:
```python
import functools

import jax
import jax.numpy as jnp
from jax import lax
from jax.experimental import pallas as pl
from jax.experimental.pallas import tpu as pltpu
from jax.sharding import PartitionSpec as P

CHUNKS = 4
LINE = 4
MIB = 1024 * 1024
ROWS0 = (((0,), (0,)), ((), ()))


def params(mib):
    return pltpu.CompilerParams(vmem_limit_bytes=mib * MIB)


def apply_kernel(first, live_ref, block_ref, values_ref, mass_ref, out_ref):
    slot = first + pl.program_id(0)
    values = values_ref[0]
    product = jnp.dot(block_ref[0], values, preferred_element_type=jnp.float32)
    nodes, width = values.shape
    weights = jnp.broadcast_to(mass_ref[pl.ds(slot, 1), :], (width, nodes)).T
    product = product + weights * values.astype(jnp.float32)
    out_ref[...] = jnp.where(slot < live_ref[0], product, 0.0).astype(jnp.bfloat16)


def apply_chunk(live, stiffness, panel, mass, first, count):
    nodes, width = panel.shape[1:]
    return pl.pallas_call(
        functools.partial(apply_kernel, first),
        grid_spec=pltpu.PrefetchScalarGridSpec(
            num_scalar_prefetch=1,
            grid=(count,),
            in_specs=[
                pl.BlockSpec((1, nodes, nodes), lambda i, s: (first + i, 0, 0)),
                pl.BlockSpec((1, nodes, width), lambda i, s: (first + i, 0, 0)),
                pl.BlockSpec(mass.shape, lambda i, s: (0, 0)),
            ],
            out_specs=pl.BlockSpec((nodes, width), lambda i, s: (i, 0)),
        ),
        out_shape=jax.ShapeDtypeStruct((count * nodes, width), jnp.bfloat16),
        compiler_params=params(16),
        cost_estimate=pl.CostEstimate(
            flops=2 * count * nodes * nodes * width,
            bytes_accessed=2 * count * nodes * (nodes + 2 * width),
            transcendentals=0,
        ),
        name="apply",
    )(live, stiffness, panel, mass)


def take_rows(rows_ref, table_ref, out_ref, count, start=0):
    group = 16

    def body(step, carry):
        base = pl.multiple_of(step * group, group)
        loaded = [table_ref[pl.ds(rows_ref[start + base + j], 1), :] for j in range(group)]
        out_ref[pl.ds(base, group), :] = jnp.concatenate(loaded, axis=0)
        return carry

    lax.fori_loop(0, count // group, body, 0)


def pick_kernel(steps, rows_ref, in_ref, prev_ref, next_ref, table, taken):
    step = pl.program_id(0)
    size = in_ref.shape[0]
    table[pl.ds(pl.multiple_of(step * size, size), size), :] = in_ref[...].astype(jnp.float32)

    @pl.when(step == steps - 1)
    def _():
        count = taken.shape[0]
        take_rows(rows_ref, table, taken, count)
        prev_ref[...] = taken[...].astype(jnp.bfloat16)
        take_rows(rows_ref, table, taken, count, count)
        next_ref[...] = taken[...].astype(jnp.bfloat16)


def pick_resident(lists, resident):
    total, width = resident.shape
    count = lists.shape[0] // 2
    steps = 8
    return pl.pallas_call(
        functools.partial(pick_kernel, steps),
        grid_spec=pltpu.PrefetchScalarGridSpec(
            num_scalar_prefetch=1,
            grid=(steps,),
            in_specs=[pl.BlockSpec((total // steps, width), lambda i, s: (i, 0))],
            out_specs=[pl.BlockSpec((count, width), lambda i, s: (0, 0))] * 2,
            scratch_shapes=[pltpu.VMEM((total, width), jnp.float32), pltpu.VMEM((count, width), jnp.float32)],
        ),
        out_shape=[jax.ShapeDtypeStruct((count, width), jnp.bfloat16)] * 2,
        compiler_params=params(48),
        cost_estimate=pl.CostEstimate(flops=0, bytes_accessed=2 * total * width * 2, transcendentals=0),
        name="pick_resident",
    )(lists, resident)


def edge_kernel(pieces, rows_ref, place_ref, *refs):
    ins, out_ref, table, taken = refs[:pieces], refs[pieces], refs[pieces + 1], refs[pieces + 2]
    size = ins[0].shape[0]
    for j in range(pieces):
        table[pl.ds(pl.multiple_of(place_ref[j] * size, size), size), :] = ins[j][...].astype(jnp.float32)
    table[pl.ds(pieces * size, 8), :] = jnp.zeros((8, table.shape[1]), jnp.float32)
    take_rows(rows_ref, table, taken, taken.shape[0])
    out_ref[...] = taken[...].astype(jnp.bfloat16)


def pick_edge(rows, places, pieces):
    size, width = pieces[0].shape
    count = rows.shape[0]
    return pl.pallas_call(
        functools.partial(edge_kernel, len(pieces)),
        grid_spec=pltpu.PrefetchScalarGridSpec(
            num_scalar_prefetch=2,
            grid=(1,),
            in_specs=[pl.BlockSpec((size, width), lambda i, s, t: (0, 0))] * len(pieces),
            out_specs=pl.BlockSpec((count, width), lambda i, s, t: (0, 0)),
            scratch_shapes=[
                pltpu.VMEM((len(pieces) * size + 8, width), jnp.float32),
                pltpu.VMEM((count, width), jnp.float32),
            ],
        ),
        out_shape=jax.ShapeDtypeStruct((count, width), jnp.bfloat16),
        compiler_params=params(24),
        cost_estimate=pl.CostEstimate(flops=0, bytes_accessed=4 * len(pieces) * size * width, transcendentals=0),
        name="pick_edge",
    )(rows, places, *pieces)


def gram_kernel(pieces, place_ref, left_ref, *refs):
    ins, total_ref, out_ref = refs[:pieces], refs[pieces], refs[pieces + 1]
    step = pl.program_id(0)

    @pl.when(step == 0)
    def _():
        out_ref[...] = total_ref[...]

    for j in range(pieces):

        @pl.when(step == j)
        def _(j=j):
            out_ref[...] += lax.dot_general(left_ref[...], ins[j][...], ROWS0, preferred_element_type=jnp.float32)


def gram_of(places, resident, pieces, total):
    size, width = pieces[0].shape
    columns = resident.shape[1]
    return pl.pallas_call(
        functools.partial(gram_kernel, len(pieces)),
        grid_spec=pltpu.PrefetchScalarGridSpec(
            num_scalar_prefetch=1,
            grid=(len(pieces),),
            in_specs=[pl.BlockSpec((size, columns), lambda i, s: (s[i], 0))]
            + [pl.BlockSpec((size, width), lambda i, s: (0, 0))] * len(pieces)
            + [pl.BlockSpec((columns, width), lambda i, s: (0, 0))],
            out_specs=pl.BlockSpec((columns, width), lambda i, s: (0, 0)),
        ),
        out_shape=jax.ShapeDtypeStruct((columns, width), jnp.float32),
        compiler_params=params(24),
        cost_estimate=pl.CostEstimate(
            flops=2 * len(pieces) * size * columns * width,
            bytes_accessed=2 * len(pieces) * size * (columns + width),
            transcendentals=0,
        ),
        name="gram_of",
    )(places, resident, *pieces, total)


def last_kernel(pieces, late, rows_ref, place_ref, left_ref, prev_ref, next_ref, total_ref, *refs):
    ins, out_ref, table, taken = refs[:pieces], refs[pieces], refs[pieces + 1], refs[pieces + 2]
    step = pl.program_id(0)
    size = ins[0].shape[0]
    count = taken.shape[0]

    @pl.when(step == 0)
    def _():
        for j in range(pieces):
            table[pl.ds(pl.multiple_of(place_ref[j] * size, size), size), :] = ins[j][...].astype(jnp.float32)
        take_rows(rows_ref, table, taken, count)
        got = taken[...].astype(jnp.bfloat16)
        out_ref[...] = total_ref[...] + lax.dot_general(prev_ref[...], got, ROWS0, preferred_element_type=jnp.float32)
        take_rows(rows_ref, table, taken, count, count)
        got = taken[...].astype(jnp.bfloat16)
        out_ref[...] += lax.dot_general(next_ref[...], got, ROWS0, preferred_element_type=jnp.float32)

    for j in range(late):

        @pl.when(step == j)
        def _(j=j):
            out_ref[...] += lax.dot_general(left_ref[...], ins[j][...], ROWS0, preferred_element_type=jnp.float32)


def gram_last(lists, places, resident, from_prev, from_next, total, pieces, late):
    size, width = pieces[0].shape
    columns = resident.shape[1]
    count = lists.shape[0] // 2
    whole = lambda shape: pl.BlockSpec(shape, lambda i, s, t: (0, 0))
    return pl.pallas_call(
        functools.partial(last_kernel, len(pieces), late),
        grid_spec=pltpu.PrefetchScalarGridSpec(
            num_scalar_prefetch=2,
            grid=(late,),
            in_specs=[
                pl.BlockSpec((size, columns), lambda i, s, t: (t[i], 0)),
                whole((count, columns)),
                whole((count, columns)),
                whole((columns, width)),
            ]
            + [whole((size, width))] * len(pieces),
            out_specs=whole((columns, width)),
            scratch_shapes=[
                pltpu.VMEM((len(pieces) * size, width), jnp.float32),
                pltpu.VMEM((count, width), jnp.float32),
            ],
        ),
        out_shape=jax.ShapeDtypeStruct((columns, width), jnp.float32),
        compiler_params=params(44),
        cost_estimate=pl.CostEstimate(
            flops=2 * (late * size + 2 * count) * columns * width,
            bytes_accessed=2 * (len(pieces) * size * width + 2 * count * columns),
            transcendentals=0,
        ),
        name="gram_last",
    )(lists, places, resident, from_prev, from_next, total, *pieces)


def shards(panel, stiffness, mass, resident, face_rows, counts):
    slots, nodes, width = panel.shape[1:]
    cols, rows = lax.axis_size("col"), lax.axis_size("row")
    column, row = lax.axis_index("col"), lax.axis_index("row")
    both = ("col", "row")
    resident = resident[0]
    columns = resident.shape[1]
    lists = face_rows[0].reshape(-1)
    count = lists.shape[0] // 2
    size = slots * nodes // CHUNKS

    def permute(value, move):
        pairs = []
        for source in range(cols * rows):
            target = move(*divmod(source, rows))
            if target is not None:
                pairs.append((source, target[0] * rows + target[1]))
        return lax.ppermute(value, both, pairs)

    across = lambda value: permute(value, lambda c, r: (c ^ 2, r))
    sibling = lambda value: permute(value, lambda c, r: (c ^ 1, r))

    live = (counts - column * slots).astype(jnp.int32)
    per = slots // CHUNKS
    own = [apply_chunk(live, stiffness[0], panel[0], mass[0], k * per, per) for k in range(CHUNKS)]
    far = [across(piece) for piece in own]
    mate = [sibling(piece) for piece in own]
    far_mate = [sibling(piece) for piece in far]

    prev_out, next_out = pick_resident(lists, resident)
    from_prev = permute(next_out, lambda c, r: (c, r + 1) if r % LINE != LINE - 1 else None)
    from_next = permute(prev_out, lambda c, r: (c, r - 1) if r % LINE != 0 else None)

    first = row % LINE == 0
    half = count // 2
    edge_rows = jnp.where(first, face_rows[0, 0], face_rows[0, 1])
    edge_rows = lax.dynamic_slice_in_dim(edge_rows, (column % 2) * half, half, 0)
    edge_rows = edge_rows - (column // 2) * (2 * slots * nodes)
    edge_rows = jnp.where((edge_rows >= 0) & (edge_rows < 2 * slots * nodes), edge_rows, 2 * slots * nodes)
    steps = jnp.arange(CHUNKS, dtype=jnp.int32)
    place = lambda c: c * CHUNKS + steps
    core = column % 2
    edge = pick_edge(edge_rows, jnp.concatenate([place(core), place(1 - core)]), own + mate)

    def beside(c, r):
        if r % LINE == LINE - 1 and r + 1 < rows:
            return c, r + 1
        if r % LINE == 0 and r > 0:
            return c, r - 1
        return None

    def crossed(c, r):
        target = beside(c, r)
        return target if target is None else (target[0] ^ 2, target[1])

    met = permute(edge, beside) + permute(edge, crossed)
    other = sibling(met)
    meeting = jnp.where(first, prev_out, next_out)
    front, back = meeting[:half], meeting[half:]
    mine = jnp.where(core == 0, front, back)
    theirs = jnp.where(core == 0, back, front)
    dot = lambda a, b: lax.dot_general(a, b, ROWS0, preferred_element_type=jnp.float32)
    total = dot(mine, met) + dot(theirs, other)

    total = gram_of(jnp.concatenate([place(column), place(column ^ 1)]), resident, own + mate, total)
    for k in range(CHUNKS - 1):
        here = jnp.stack([(column ^ 2) * CHUNKS + k, (column ^ 3) * CHUNKS + k])
        total = gram_of(here, resident, [far[k], far_mate[k]], total)
    k = CHUNKS - 1
    order = jnp.stack([(column ^ 2) * CHUNKS + k, (column ^ 3) * CHUNKS + k])
    order = jnp.concatenate([order, place(column ^ 2)[:k], place(column ^ 3)[:k], place(column), place(column ^ 1)])
    pieces = [far[k], far_mate[k]] + far[:k] + far_mate[:k] + own + mate
    gram = gram_last(lists, order, resident, from_prev, from_next, total, pieces, 2)

    own_rows = columns // rows
    received = lax.all_to_all(gram.reshape(rows, own_rows, width), "row", 0, 0)
    return jnp.sum(received, axis=0)


def solution(mesh):
    in_specs = (
        P("row", "col", None, None),
        P("row", "col", None, None),
        P("row", "col", None),
        P("row", None, "col"),
        P("row", None, None),
        P("row"),
    )
    out_specs = P(("col", "row"), None)
    return jax.shard_map(shards, mesh=mesh, in_specs=in_specs, out_specs=out_specs, check_vma=False)
```

time: 439 us -> 123 us (0.28)
  waiting for transfers between devices: 333 us -> 20.1 us
  Pallas kernels: 0 us -> 45.5 us
  other arithmetic: 46.4 us -> 6.29 us
  blocking collectives: 0 us -> 15.7 us
  matrix products: 17.5 us -> 3.25 us
  between operations: 14.1 us -> 0.95 us
  starting transfers between devices: 5.91 us -> 17.5 us
  local copies, waits for them, and re-layouts: 20.7 us -> 12.8 us
    psum x1 -> x0, waiting for transfers between devices: 281 us -> none  [shards(): full_gram = lax.psum(partial_gram, 'row')]
    all_gather x1 -> x0, waiting for transfers between devices: 52.9 us -> none  [shards(): whole = lax.all_gather(local_rows, 'col', axis=0, tiled=True)]
    pallas_call x0 -> x11, Pallas kernels: none -> 45.5 us  [the longest x1 17.3 us: pick_resident(): pl.pallas_call(functools.partial(pick_kernel, steps), grid_spec=pltpu.Pre...]
    scatter-add x2 -> x0, other arithmetic: 39 us -> none  [the longest x1 19.5 us: shards(): summed = summed.at[prev_rows].add(from_prev.astype(jnp.float32))]
    ppermute x2 -> x17, waiting for transfers between devices: 0.01 us -> 20.1 us  [permute(): return lax.ppermute(value, both, pairs)]
    gather x2 -> x0, local copies, waits for them, and re-layouts: 18.4 us -> none  [the longest x1 9.19 us: shards(): from_prev = passed_along(whole[next_rows], 'row', 1)]
    all_to_all x0 -> x1, blocking collectives: none -> 15.7 us  [shards(): received = lax.all_to_all(gram.reshape(rows, own_rows, width), 'row', 0, 0)]
    dot_general x2, matrix products: 17.5 us -> 3.25 us  [shards(): lax.dot_general(a, b, ROWS0, preferred_element_type=jnp.float32)]
  transfers between devices with their start and end apart: 4 -> 17, of which waited for: 2 -> 3; matrix products, arithmetic and copies ran while one was open for 8% -> 9% of each run, Pallas kernels for 0% -> 28%
where the time goes in v2:
time: 123 us; the launch traced here: 122 us
  Pallas kernels  45.5 us (37%)
  waiting for transfers between devices  20.1 us (16%)
  starting transfers between devices  17.5 us (14%)
  blocking collectives  15.7 us (13%)
  local copies, waits for them, and re-layouts  12.8 us (10%)
  other arithmetic  6.29 us (5%)
  matrix products  3.25 us (3%)
    ppermute x17, waiting for transfers between devices, permute(): return lax.ppermute(value, both, pairs)  20.1 us
    ppermute x17, starting transfers between devices, permute(): return lax.ppermute(value, both, pairs)  17.5 us
    pallas_call x1, Pallas kernels, pick_resident(): pl.pallas_call(functools.partial(pick_kernel, steps), grid_spec=pltpu.Pre...  17.3 us
    all_to_all x1, blocking collectives, shards(): received = lax.all_to_all(gram.reshape(rows, own_rows, width), 'row', 0, 0)  15.7 us
    pallas_call x4, Pallas kernels, gram_of(): pl.pallas_call(functools.partial(gram_kernel, len(pieces)), grid_spec=plt...  11.4 us
    unnamed x28, local copies, waits for them, and re-layouts  10.9 us
    pallas_call x1, Pallas kernels, gram_last(): pl.pallas_call(functools.partial(last_kernel, len(pieces), late), grid_sp...  10.1 us
    pallas_call x4, Pallas kernels, apply_chunk(): pl.pallas_call(functools.partial(apply_kernel, first), grid_spec=pltpu.Pr...  3.77 us
  transfers between devices with their start and end apart: 17, of which 3 were waited for; matrix products, arithmetic and copies ran while one was open for 9% of the time, Pallas kernels for 28%

profile of v2, /device:TPU:0, one launch (start us, length us, event | category | flops | bytes accessed | tf_op | source)
XLA Modules:
  0.0 122.1 jit_solution(11653503186411271362)
XLA Ops:
  0.7 0.7 copy.10
  1.4 2.8 %copy-done.1 = bf16[1,12,512,512]{3,2,1,0:T(8,128)(2,1)S(1)} copy-done((bf16[1,12,512,512]{3,2,1,0:T(8,128)(2,1)S(1)}, bf16[1,12,512,512]{3,2,1,0:T(8,128)(2,1)}, u32[]{:S(2)}) %copy-start.1) | copy-done | bytes 6291480
  4.2 1.4 %copy-done.2 = bf16[1,12,512,128]{3,2,1,0:T(8,128)(2,1)S(1)} copy-done((bf16[1,12,512,128]{3,2,1,0:T(8,128)(2,1)S(1)}, bf16[1,12,512,128]{3,2,1,0:T(8,128)(2,1)}, u32[]{:S(2)}) %copy-start.2) | copy-done | bytes 1572888
  5.6 0.9 apply.6.refs_0_.refs_8_
  6.5 0.1 collective-permute-start.8
  6.6 3.4 %collective-permute-start.6 = (bf16[1536,128]{1,0:T(8,128)(2,1)S(1)}, bf16[1536,128]{1,0:T(8,128)(2,1)S(1)}, u32[]{:S(2)}, u32[]{:S(2)}) collective-permute-start(bf16[1536,128]{1,0:T(8,128)(2,1)S(1)} %apply.6.refs_0_.refs_8_), channel_id=1, source_target_pairs={{0,64},{1,65},{2,66},{3,67},{4,68},{5,69},{6,70},{7,71},{8,72},{9,... | collective-permute-start | bytes 1179656 | tf_op jit(solution)/shard_map/ppermute | solution.py:247
  10.0 0.9 apply.4.refs_2_.refs_10_
  10.9 0.0 copy-start.8
  11.0 0.2 collective-permute-start.10
  11.2 0.9 apply.7.refs_3_.refs_11_
  12.1 0.4 collective-permute-start.11
  12.6 0.9 apply.5.refs_1_.refs_9_
  13.5 0.2 collective-permute-start.9
  13.8 0.6 fusion.10
  14.4 0.7 copy.8
  15.1 17.3 %pick_resident.1 = (bf16[2048,256]{1,0:T(8,128)(2,1)S(1)}, bf16[2048,256]{1,0:T(8,128)(2,1)S(1)}) custom-call(s32[4096]{0:T(1024)S(1)} %bitcast.42, bf16[24576,256]{1,0:T(8,128)(2,1)} %bitcast.23), custom_call_target="tpu_custom_call" | custom-call | bytes 25165824 | tf_op jit(solution)/shard_map/pick_resident/pallas_call | solution.py:85
  32.5 1.2 %broadcast_select_fusion = bf16[2048,256]{1,0:T(8,128)(2,1)} fusion(bf16[2048,256]{1,0:T(8,128)(2,1)S(1)} %get-tuple-element.8, bf16[2048,256]{1,0:T(8,128)(2,1)S(1)} %get-tuple-element.7, pred[]{:T(512)S(6)} %eq.12), kind=kLoop, calls=%fused_computation.1 | loop fusion | flops 524288 | bytes 3145729 | tf_op jit(solution)/shard_map/jit(_where)/select_n | solution.py:287
  33.7 0.0 collective-permute-done.10.refs_6_.refs_14_
  33.7 0.3 collective-permute-start.4
  34.1 0.1 pad_add_fusion.4.place_ref
  34.2 0.0 collective-permute-done.11.refs_7_.refs_15_
  34.2 3.3 %collective-permute-start.2 = (bf16[1536,128]{1,0:T(8,128)(2,1)S(1)}, bf16[1536,128]{1,0:T(8,128)(2,1)}, u32[]{:S(2)}, u32[]{:S(2)}) collective-permute-start(bf16[1536,128]{1,0:T(8,128)(2,1)S(1)} %apply.4.refs_2_.refs_10_), channel_id=1, source_target_pairs={{0,64},{1,65},{2,66},{3,67},{4,68},{5,69},{6,70},{7,71},{8,72},{9,... | collective-permute-start | bytes 1179656 | tf_op jit(solution)/shard_map/ppermute | solution.py:247
  37.5 0.0 collective-permute-done.8.refs_4_.refs_12_
  37.5 0.0 collective-permute-done.9.refs_5_.refs_13_
  37.5 2.9 %pick_edge.1 = bf16[1024,128]{1,0:T(8,128)(2,1)} custom-call(s32[1024]{0:T(1024)S(1)} %and_select_fusion.rows_ref, s32[8]{0:T(128)S(1)} %pad_add_fusion.4.place_ref, bf16[1536,128]{1,0:T(8,128)(2,1)S(1)} %apply.6.refs_0_.refs_8_, bf16[1536,128]{1,0:T(8,128)(2,1)S(1)} %apply.5.refs_1_.refs_9_, bf16[1536,128]{1,0:T(8,128)(2,1)S(1)} %apply.4.refs_2_.refs_10_, ...), custom_call_target="tpu_custom_call" | custom-call | bytes 6291456 | tf_op jit(solution)/shard_map/pick_edge/pallas_call | solution.py:114
  40.4 1.3 %collective-permute-start.12 = (bf16[1024,128]{1,0:T(8,128)(2,1)}, bf16[1024,128]{1,0:T(8,128)(2,1)}, u32[]{:S(2)}, u32[]{:S(2)}) collective-permute-start(bf16[1024,128]{1,0:T(8,128)(2,1)} %pick_edge.1), channel_id=1, source_target_pairs={{3,4},{4,3},{7,8},{8,7},{11,12},{12,11},{15,16},{16,15},{19,20},{2... | collective-permute-start | bytes 786440 | tf_op jit(solution)/shard_map/ppermute | solution.py:247
  41.8 1.4 %collective-permute-start.13 = (bf16[1024,128]{1,0:T(8,128)(2,1)}, bf16[1024,128]{1,0:T(8,128)(2,1)}, u32[]{:S(2)}, u32[]{:S(2)}) collective-permute-start(bf16[1024,128]{1,0:T(8,128)(2,1)} %pick_edge.1), channel_id=1, source_target_pairs={{3,68},{4,67},{7,72},{8,71},{11,76},{12,75},{15,80},{16,79},{19,84... | collective-permute-start | bytes 786440 | tf_op jit(solution)/shard_map/ppermute | solution.py:247
  43.1 0.5 iota_add_fusion.5
  43.6 0.6 iota_add_fusion.4
  44.2 0.3 collective-permute-start.15
  44.5 2.8 %collective-permute-done.4.refs_0_.refs_3_ = bf16[1536,128]{1,0:T(8,128)(2,1)} collective-permute-done((bf16[1536,128]{1,0:T(8,128)(2,1)S(1)}, bf16[1536,128]{1,0:T(8,128)(2,1)}, u32[]{:S(2)}, u32[]{:S(2)}) %collective-permute-start.4) | collective-permute-done | bytes 393248 | tf_op jit(solution)/shard_map/ppermute | solution.py:247
  47.4 4.4 %collective-permute-start = (bf16[2048,256]{1,0:T(8,128)(2,1)}, bf16[2048,256]{1,0:T(8,128)(2,1)}, u32[]{:S(2)}, u32[]{:S(2)}) collective-permute-start(bf16[2048,256]{1,0:T(8,128)(2,1)} %copy-done.4), channel_id=1, source_target_pairs={{0,1},{1,2},{2,3},{4,5},{5,6},{6,7},{8,9},{9,10},{10,11},{12,13},{... | collective-permute-start | bytes 3145736 | tf_op jit(solution)/shard_map/ppermute | solution.py:247
  51.7 0.0 collective-permute-done.12
  51.7 1.3 %collective-permute-start.1 = (bf16[2048,256]{1,0:T(8,128)(2,1)}, bf16[2048,256]{1,0:T(8,128)(2,1)}, u32[]{:S(2)}, u32[]{:S(2)}) collective-permute-start(bf16[2048,256]{1,0:T(8,128)(2,1)} %copy-done.3), channel_id=1, source_target_pairs={{1,0},{2,1},{3,2},{5,4},{6,5},{7,6},{9,8},{10,9},{11,10},{13,12},{... | collective-permute-start | bytes 3145736 | tf_op jit(solution)/shard_map/ppermute | solution.py:247
  53.0 0.0 collective-permute-done.13
  53.0 0.1 collective-permute-start.7
  53.2 0.6 pad_add_fusion.3.place_ref
  53.8 1.8 %add.97 = bf16[1024,128]{1,0:T(8,128)(2,1)} add(bf16[1024,128]{1,0:T(8,128)(2,1)} %collective-permute-done.12, bf16[1024,128]{1,0:T(8,128)(2,1)} %collective-permute-done.13) | non-fusion elementwise | flops 131072 | bytes 786432 | tf_op jit(solution)/shard_map/add | solution.py:285
  55.6 11.4 %collective-permute-done.2.refs_0_.refs_4_ = bf16[1536,128]{1,0:T(8,128)(2,1)} collective-permute-done((bf16[1536,128]{1,0:T(8,128)(2,1)S(1)}, bf16[1536,128]{1,0:T(8,128)(2,1)}, u32[]{:S(2)}, u32[]{:S(2)}) %collective-permute-start.2) | collective-permute-done | bytes 393248 | tf_op jit(solution)/shard_map/ppermute | solution.py:247
  67.0 0.6 pad_add_fusion.2.place_ref
  67.7 1.3 %concatenate.9.place_ref = s32[16]{0:T(128)} concatenate(s32[1]{0:T(128)} %bitcast, s32[1]{0:T(128)} %bitcast.1, s32[3]{0:T(128)} %bitcast.46, s32[3]{0:T(128)} %bitcast.47, s32[4]{0:T(128)} %copy-done.12, s32[4]{0:T(128)} %copy-done.11), dimensions={0} | concatenate | bytes 128 | tf_op jit(solution)/shard_map/concatenate | solution.py:300
  69.0 0.1 pad_add_fusion.1.place_ref
  69.0 0.1 pad_add_fusion.place_ref
  69.1 5.8 %collective-permute-done.15.refs_0_ = bf16[1536,128]{1,0:T(8,128)(2,1)} collective-permute-done((bf16[1536,128]{1,0:T(8,128)(2,1)S(1)}, bf16[1536,128]{1,0:T(8,128)(2,1)}, u32[]{:S(2)}, u32[]{:S(2)}) %collective-permute-start.15) | collective-permute-done | bytes 393248 | tf_op jit(solution)/shard_map/ppermute | solution.py:247
  74.9 0.0 collective-permute-start.5
  74.9 0.0 collective-permute-done.7.refs_1_.refs_5_
  74.9 0.5 collective-permute-start.3
  75.4 0.0 collective-permute-done.14
  75.4 0.3 collective-permute-start.16
  75.7 1.6 %fusion = f32[256,128]{1,0:T(8,128)S(1)} fusion(bf16[1024,128]{1,0:T(8,128)(2,1)} %collective-permute-done.14, pred[]{:T(512)S(6)} %eq.11, bf16[2048,256]{1,0:T(8,128)(2,1)} %broadcast_select_fusion), kind=kOutput, calls=%fused_computation.2 | convolution fusion | flops 67371008 | bytes 1441793 | tf_op jit(solution)/shard_map/dot_general | solution.py:291
  77.3 1.6 %convolution_add_fusion.refs_8_ = f32[256,128]{1,0:T(8,128)S(1)} fusion(f32[256,128]{1,0:T(8,128)S(1)} %fusion, bf16[1024,128]{1,0:T(8,128)(2,1)} %add.97, pred[]{:T(512)S(6)} %eq.11, bf16[2048,256]{1,0:T(8,128)(2,1)} %broadcast_select_fusion), kind=kOutput, calls=%fused_computation | convolution fusion | flops 67403776 | bytes 1572865 | tf_op jit(solution)/shard_map/dot_general | solution.py:291
  78.9 0.0 copy-start
  79.0 4.6 %copy-done = bf16[1,24576,256]{2,1,0:T(8,128)(2,1)S(1)} copy-done((bf16[1,24576,256]{2,1,0:T(8,128)(2,1)S(1)}, bf16[1,24576,256]{2,1,0:T(8,128)(2,1)}, u32[]{:S(2)}) %copy-start) | copy-done | bytes 12582936
  83.5 0.7 copy-done.6
  84.2 4.2 %gram_of.4.refs_2_ = f32[256,128]{1,0:T(8,128)S(1)} custom-call(s32[8]{0:T(128)S(1)} %copy-done.6, bf16[24576,256]{1,0:T(8,128)(2,1)S(1)} %bitcast.25, bf16[1536,128]{1,0:T(8,128)(2,1)S(1)} %apply.6.refs_0_.refs_8_, bf16[1536,128]{1,0:T(8,128)(2,1)S(1)} %apply.5.refs_1_.refs_9_, bf16[1536,128]{1,0:T(8,128)(2,1)S(1)} %apply.4.refs_2_.refs_10_, ...), custom_call_target="tpu_custom_call" | custom-call | flops 805306368 | bytes 9437184 | tf_op jit(solution)/shard_map/gram_of/pallas_call | solution.py:151
  88.4 2.4 %gram_of.5.refs_2_ = f32[256,128]{1,0:T(8,128)S(1)} custom-call(s32[2]{0:T(128)S(1)} %copy-done.7, bf16[24576,256]{1,0:T(8,128)(2,1)S(1)} %bitcast.26, bf16[1536,128]{1,0:T(8,128)(2,1)S(1)} %collective-permute-done.6.refs_0_.refs_2_, bf16[1536,128]{1,0:T(8,128)(2,1)} %collective-permute-done.7.refs_1_.refs_5_, f32[256,128]{1,0:T(8,128)S(1)} %gram_of.4.refs_2_), custom_call_target="tpu_custom_call" | custom-call | flops 201326592 | bytes 2359296 | tf_op jit(solution)/shard_map/gram_of/pallas_call | solution.py:151
  90.8 2.4 %gram_of.6.refs_2_ = f32[256,128]{1,0:T(8,128)S(1)} custom-call(s32[2]{0:T(128)S(1)} %pad_add_fusion.1.place_ref, bf16[24576,256]{1,0:T(8,128)(2,1)S(1)} %bitcast.27, bf16[1536,128]{1,0:T(8,128)(2,1)} %collective-permute-done.4.refs_0_.refs_3_, bf16[1536,128]{1,0:T(8,128)(2,1)S(1)} %collective-permute-done.5.refs_1_.refs_6_, f32[256,128]{1,0:T(8,128)S(1)} %gram_of.5.refs_2_), custom_call_target="tpu_custom_call" | custom-call | flops 201326592 | bytes 2359296 | tf_op jit(solution)/shard_map/gram_of/pallas_call | solution.py:151
  93.2 0.0 collective-permute-done.3.refs_1_.refs_7_
  93.2 2.4 %gram_of.7.total_ref = f32[256,128]{1,0:T(8,128)S(1)} custom-call(s32[2]{0:T(128)S(1)} %pad_add_fusion.place_ref, bf16[24576,256]{1,0:T(8,128)(2,1)S(1)} %bitcast.28, bf16[1536,128]{1,0:T(8,128)(2,1)} %collective-permute-done.2.refs_0_.refs_4_, bf16[1536,128]{1,0:T(8,128)(2,1)S(1)} %collective-permute-done.3.refs_1_.refs_7_, f32[256,128]{1,0:T(8,128)S(1)} %gram_of.6.refs_2_), custom_call_target="tpu_custom_call" | custom-call | flops 201326592 | bytes 2359296 | tf_op jit(solution)/shard_map/gram_of/pallas_call | solution.py:151
  95.6 0.0 collective-permute-done.16.refs_1_
  95.7 0.0 collective-permute-done.prev_ref
  95.7 10.1 %gram_last.1 = f32[256,128]{1,0:T(8,128)S(1)} custom-call(s32[4096]{0:T(1024)S(1)} %bitcast.43, s32[16]{0:T(128)S(1)} %copy-done.5, bf16[24576,256]{1,0:T(8,128)(2,1)} %bitcast.24, bf16[2048,256]{1,0:T(8,128)(2,1)} %collective-permute-done.prev_ref, bf16[2048,256]{1,0:T(8,128)(2,1)} %collective-permute-done.1.next_ref, f32[256,128]{1,0:T(8,128)S(1)} %gram_of.7.total_ref, ...), custom_call_target="tpu_custom_call" | custom-call | flops 469762048 | bytes 8388608 | tf_op jit(solution)/shard_map/gram_last/pallas_call | solution.py:201
  105.8 15.7 %all_to_all.5 = f32[32,8,128]{2,1,0:T(8,128)S(1)} all-to-all(f32[32,8,128]{2,1,0:T(8,128)S(1)} %bitcast.41), channel_id=1, replica_groups=mesh['col'=4,'row'=32] {'row'}, dimensions={0} | all-to-all | bytes 262144 | tf_op jit(solution)/shard_map/all_to_all | solution.py:305
  121.5 0.6 reduce_sum.9
  (28 shorter events, 0.1 us)
Async XLA Ops:
  1.4 2.8 %copy-start.1 = (bf16[1,12,512,512]{3,2,1,0:T(8,128)(2,1)S(1)}, bf16[1,12,512,512]{3,2,1,0:T(8,128)(2,1)}, u32[]{:S(2)}) copy-start(bf16[1,12,512,512]{3,2,1,0:T(8,128)(2,1)} %param.7) | copy-start | bytes 18874372
  4.2 1.4 %copy-start.2 = (bf16[1,12,512,128]{3,2,1,0:T(8,128)(2,1)S(1)}, bf16[1,12,512,128]{3,2,1,0:T(8,128)(2,1)}, u32[]{:S(2)}) copy-start(bf16[1,12,512,128]{3,2,1,0:T(8,128)(2,1)} %param.6) | copy-start | bytes 4718596
  6.5 30.9 %collective-permute-start.8 = (bf16[1536,128]{1,0:T(8,128)(2,1)S(1)}, bf16[1536,128]{1,0:T(8,128)(2,1)S(1)}, u32[]{:S(2)}, u32[]{:S(2)}) collective-permute-start(bf16[1536,128]{1,0:T(8,128)(2,1)S(1)} %apply.6.refs_0_.refs_8_), channel_id=1, source_target_pairs={{0,32},{1,33},{2,34},{3,35},{4,36},{5,37},{6,38},{7,39},{8,40},{9,... | collective-permute-start | bytes 1179656 | tf_op jit(solution)/shard_map/ppermute | solution.py:247
  6.6 37.6 %collective-permute-start.6 = (bf16[1536,128]{1,0:T(8,128)(2,1)S(1)}, bf16[1536,128]{1,0:T(8,128)(2,1)S(1)}, u32[]{:S(2)}, u32[]{:S(2)}) collective-permute-start(bf16[1536,128]{1,0:T(8,128)(2,1)S(1)} %apply.6.refs_0_.refs_8_), channel_id=1, source_target_pairs={{0,64},{1,65},{2,66},{3,67},{4,68},{5,69},{6,70},{7,71},{8,72},{9,... | collective-permute-start | bytes 1179656 | tf_op jit(solution)/shard_map/ppermute | solution.py:247
  10.9 2.8 %copy-start.8 = (s32[1,2,2048]{2,1,0:T(2,128)S(1)}, s32[1,2,2048]{2,1,0:T(2,128)}, u32[]{:S(2)}) copy-start(s32[1,2,2048]{2,1,0:T(2,128)} %param.10) | copy-start | bytes 49156
  11.0 22.8 %collective-permute-start.10 = (bf16[1536,128]{1,0:T(8,128)(2,1)S(1)}, bf16[1536,128]{1,0:T(8,128)(2,1)S(1)}, u32[]{:S(2)}, u32[]{:S(2)}) collective-permute-start(bf16[1536,128]{1,0:T(8,128)(2,1)S(1)} %apply.4.refs_2_.refs_10_), channel_id=1, source_target_pairs={{0,32},{1,33},{2,34},{3,35},{4,36},{5,37},{6,38},{7,39},{8,40},{9,... | collective-permute-start | bytes 1179656 | tf_op jit(solution)/shard_map/ppermute | solution.py:247
  12.1 22.0 %collective-permute-start.11 = (bf16[1536,128]{1,0:T(8,128)(2,1)S(1)}, bf16[1536,128]{1,0:T(8,128)(2,1)S(1)}, u32[]{:S(2)}, u32[]{:S(2)}) collective-permute-start(bf16[1536,128]{1,0:T(8,128)(2,1)S(1)} %apply.7.refs_3_.refs_11_), channel_id=1, source_target_pairs={{0,32},{1,33},{2,34},{3,35},{4,36},{5,37},{6,38},{7,39},{8,40},{9,... | collective-permute-start | bytes 1179656 | tf_op jit(solution)/shard_map/ppermute | solution.py:247
  13.5 23.9 %collective-permute-start.9 = (bf16[1536,128]{1,0:T(8,128)(2,1)S(1)}, bf16[1536,128]{1,0:T(8,128)(2,1)S(1)}, u32[]{:S(2)}, u32[]{:S(2)}) collective-permute-start(bf16[1536,128]{1,0:T(8,128)(2,1)S(1)} %apply.5.refs_1_.refs_9_), channel_id=1, source_target_pairs={{0,32},{1,33},{2,34},{3,35},{4,36},{5,37},{6,38},{7,39},{8,40},{9,... | collective-permute-start | bytes 1179656 | tf_op jit(solution)/shard_map/ppermute | solution.py:247
  15.1 18.6 %copy-start.9 = (s32[1,1,2048]{2,1,0:T(1,128)S(1)}, s32[1,1,2048]{2,1,0:T(1,128)}, u32[]{:S(2)}) copy-start(s32[1,1,2048]{2,1,0:T(1,128)} %get-tuple-element.9) | copy-start | bytes 24580
  15.1 18.6 %copy-start.10 = (s32[1,1,2048]{2,1,0:T(1,128)S(1)}, s32[1,1,2048]{2,1,0:T(1,128)}, u32[]{:S(2)}) copy-start(s32[1,1,2048]{2,1,0:T(1,128)} %get-tuple-element.10) | copy-start | bytes 24580
  32.4 5.0 %copy-start.4 = (bf16[2048,256]{1,0:T(8,128)(2,1)}, bf16[2048,256]{1,0:T(8,128)(2,1)S(1)}, u32[]{:S(2)}) copy-start(bf16[2048,256]{1,0:T(8,128)(2,1)S(1)} %get-tuple-element.7) | copy-start | bytes 3145732
  32.4 5.0 %copy-start.3 = (bf16[2048,256]{1,0:T(8,128)(2,1)}, bf16[2048,256]{1,0:T(8,128)(2,1)S(1)}, u32[]{:S(2)}) copy-start(bf16[2048,256]{1,0:T(8,128)(2,1)S(1)} %get-tuple-element.8) | copy-start | bytes 3145732
  33.7 13.6 %collective-permute-start.4 = (bf16[1536,128]{1,0:T(8,128)(2,1)S(1)}, bf16[1536,128]{1,0:T(8,128)(2,1)}, u32[]{:S(2)}, u32[]{:S(2)}) collective-permute-start(bf16[1536,128]{1,0:T(8,128)(2,1)S(1)} %apply.5.refs_1_.refs_9_), channel_id=1, source_target_pairs={{0,64},{1,65},{2,66},{3,67},{4,68},{5,69},{6,70},{7,71},{8,72},{9,... | collective-permute-start | bytes 1179656 | tf_op jit(solution)/shard_map/ppermute | solution.py:247
  34.2 32.9 %collective-permute-start.2 = (bf16[1536,128]{1,0:T(8,128)(2,1)S(1)}, bf16[1536,128]{1,0:T(8,128)(2,1)}, u32[]{:S(2)}, u32[]{:S(2)}) collective-permute-start(bf16[1536,128]{1,0:T(8,128)(2,1)S(1)} %apply.4.refs_2_.refs_10_), channel_id=1, source_target_pairs={{0,64},{1,65},{2,66},{3,67},{4,68},{5,69},{6,70},{7,71},{8,72},{9,... | collective-permute-start | bytes 1179656 | tf_op jit(solution)/shard_map/ppermute | solution.py:247
  40.4 11.3 %collective-permute-start.12 = (bf16[1024,128]{1,0:T(8,128)(2,1)}, bf16[1024,128]{1,0:T(8,128)(2,1)}, u32[]{:S(2)}, u32[]{:S(2)}) collective-permute-start(bf16[1024,128]{1,0:T(8,128)(2,1)} %pick_edge.1), channel_id=1, source_target_pairs={{3,4},{4,3},{7,8},{8,7},{11,12},{12,11},{15,16},{16,15},{19,20},{2... | collective-permute-start | bytes 786440 | tf_op jit(solution)/shard_map/ppermute | solution.py:247
  41.8 11.3 %collective-permute-start.13 = (bf16[1024,128]{1,0:T(8,128)(2,1)}, bf16[1024,128]{1,0:T(8,128)(2,1)}, u32[]{:S(2)}, u32[]{:S(2)}) collective-permute-start(bf16[1024,128]{1,0:T(8,128)(2,1)} %pick_edge.1), channel_id=1, source_target_pairs={{3,68},{4,67},{7,72},{8,71},{11,76},{12,75},{15,80},{16,79},{19,84... | collective-permute-start | bytes 786440 | tf_op jit(solution)/shard_map/ppermute | solution.py:247
  44.2 8.9 %copy-start.11 = (s32[4]{0:T(128)}, s32[4]{0:T(128)S(1)}, u32[]{:S(2)}) copy-start(s32[4]{0:T(128)S(1)} %get-tuple-element.11) | copy-start | bytes 52
  44.2 8.9 %copy-start.12 = (s32[4]{0:T(128)}, s32[4]{0:T(128)S(1)}, u32[]{:S(2)}) copy-start(s32[4]{0:T(128)S(1)} %get-tuple-element.12) | copy-start | bytes 52
  44.2 30.7 %collective-permute-start.15 = (bf16[1536,128]{1,0:T(8,128)(2,1)S(1)}, bf16[1536,128]{1,0:T(8,128)(2,1)}, u32[]{:S(2)}, u32[]{:S(2)}) collective-permute-start(bf16[1536,128]{1,0:T(8,128)(2,1)S(1)} %apply.7.refs_3_.refs_11_), channel_id=1, source_target_pairs={{0,64},{1,65},{2,66},{3,67},{4,68},{5,69},{6,70},{7,71},{8,72},{9,... | collective-permute-start | bytes 1179656 | tf_op jit(solution)/shard_map/ppermute | solution.py:247
  47.4 48.3 %collective-permute-start = (bf16[2048,256]{1,0:T(8,128)(2,1)}, bf16[2048,256]{1,0:T(8,128)(2,1)}, u32[]{:S(2)}, u32[]{:S(2)}) collective-permute-start(bf16[2048,256]{1,0:T(8,128)(2,1)} %copy-done.4), channel_id=1, source_target_pairs={{0,1},{1,2},{2,3},{4,5},{5,6},{6,7},{8,9},{9,10},{10,11},{12,13},{... | collective-permute-start | bytes 3145736 | tf_op jit(solution)/shard_map/ppermute | solution.py:247
  51.7 43.9 %collective-permute-start.1 = (bf16[2048,256]{1,0:T(8,128)(2,1)}, bf16[2048,256]{1,0:T(8,128)(2,1)}, u32[]{:S(2)}, u32[]{:S(2)}) collective-permute-start(bf16[2048,256]{1,0:T(8,128)(2,1)} %copy-done.3), channel_id=1, source_target_pairs={{1,0},{2,1},{3,2},{5,4},{6,5},{7,6},{9,8},{10,9},{11,10},{13,12},{... | collective-permute-start | bytes 3145736 | tf_op jit(solution)/shard_map/ppermute | solution.py:247
  53.0 21.9 %collective-permute-start.7 = (bf16[1536,128]{1,0:T(8,128)(2,1)S(1)}, bf16[1536,128]{1,0:T(8,128)(2,1)}, u32[]{:S(2)}, u32[]{:S(2)}) collective-permute-start(bf16[1536,128]{1,0:T(8,128)(2,1)S(1)} %collective-permute-done.6.refs_0_.refs_2_), channel_id=1, source_target_pairs={{0,32},{1,33},{2,34},{3,35},{4,36},{5,37},{6,38},{7,39},{8,40},{9,... | collective-permute-start | bytes 1179656 | tf_op jit(solution)/shard_map/ppermute | solution.py:247
  67.0 8.4 %collective-permute-start.14 = (bf16[1024,128]{1,0:T(8,128)(2,1)}, bf16[1024,128]{1,0:T(8,128)(2,1)}, u32[]{:S(2)}, u32[]{:S(2)}) collective-permute-start(bf16[1024,128]{1,0:T(8,128)(2,1)} %add.97), channel_id=1, source_target_pairs={{0,32},{1,33},{2,34},{3,35},{4,36},{5,37},{6,38},{7,39},{8,40},{9,... | collective-permute-start | bytes 786440 | tf_op jit(solution)/shard_map/ppermute | solution.py:247
  74.9 15.9 %collective-permute-start.5 = (bf16[1536,128]{1,0:T(8,128)(2,1)}, bf16[1536,128]{1,0:T(8,128)(2,1)S(1)}, u32[]{:S(2)}, u32[]{:S(2)}) collective-permute-start(bf16[1536,128]{1,0:T(8,128)(2,1)} %collective-permute-done.4.refs_0_.refs_3_), channel_id=1, source_target_pairs={{0,32},{1,33},{2,34},{3,35},{4,36},{5,37},{6,38},{7,39},{8,40},{9,... | collective-permute-start | bytes 1179656 | tf_op jit(solution)/shard_map/ppermute | solution.py:247
  74.9 18.3 %collective-permute-start.3 = (bf16[1536,128]{1,0:T(8,128)(2,1)}, bf16[1536,128]{1,0:T(8,128)(2,1)S(1)}, u32[]{:S(2)}, u32[]{:S(2)}) collective-permute-start(bf16[1536,128]{1,0:T(8,128)(2,1)} %collective-permute-done.2.refs_0_.refs_4_), channel_id=1, source_target_pairs={{0,32},{1,33},{2,34},{3,35},{4,36},{5,37},{6,38},{7,39},{8,40},{9,... | collective-permute-start | bytes 1179656 | tf_op jit(solution)/shard_map/ppermute | solution.py:247
  75.4 20.2 %collective-permute-start.16 = (bf16[1536,128]{1,0:T(8,128)(2,1)}, bf16[1536,128]{1,0:T(8,128)(2,1)S(1)}, u32[]{:S(2)}, u32[]{:S(2)}) collective-permute-start(bf16[1536,128]{1,0:T(8,128)(2,1)} %collective-permute-done.15.refs_0_), channel_id=1, source_target_pairs={{0,32},{1,33},{2,34},{3,35},{4,36},{5,37},{6,38},{7,39},{8,40},{9,... | collective-permute-start | bytes 1179656 | tf_op jit(solution)/shard_map/ppermute | solution.py:247
  78.9 4.6 %copy-start = (bf16[1,24576,256]{2,1,0:T(8,128)(2,1)S(1)}, bf16[1,24576,256]{2,1,0:T(8,128)(2,1)}, u32[]{:S(2)}) copy-start(bf16[1,24576,256]{2,1,0:T(8,128)(2,1)} %param.9) | copy-start | bytes 37748740
  83.5 0.7 copy-start.6
  84.2 4.2 %copy-start.7 = (s32[2]{0:T(128)S(1)}, s32[2]{0:T(128)}, u32[]{:S(2)}) copy-start(s32[2]{0:T(128)} %pad_add_fusion.2.place_ref) | copy-start | bytes 28
  93.2 2.5 %copy-start.5 = (s32[16]{0:T(128)S(1)}, s32[16]{0:T(128)}, u32[]{:S(2)}) copy-start(s32[16]{0:T(128)} %concatenate.9.place_ref) | copy-start | bytes 196

commit v3 on v0

v3 whole, which is shorter than its diff:
```python
import functools
import math

import jax
import jax.numpy as jnp
from jax import lax
from jax.experimental import pallas as pl
from jax.experimental.pallas import tpu as pltpu
from jax.sharding import PartitionSpec as P

SPLIT = (3, 1)
LINE = 4
MIB = 1024 * 1024
ROWS0 = (((0,), (0,)), ((), ()))
AXES = ("col", "row")


def params(mib):
    return pltpu.CompilerParams(vmem_limit_bytes=mib * MIB)


HBM = pl.BlockSpec(memory_space=pltpu.HBM)
ANY = pl.BlockSpec(memory_space=pl.ANY)
SMEM = pl.BlockSpec(memory_space=pltpu.SMEM)
VMEM = pl.BlockSpec(memory_space=pltpu.VMEM)


def cost(flops, moved):
    return pl.CostEstimate(flops=flops, bytes_accessed=moved, transcendentals=0)


def in_hbm(value):
    return pltpu.with_memory_space_constraint(value, pltpu.HBM)


def dot0(left, right):
    return lax.dot_general(left, right, ROWS0, preferred_element_type=jnp.float32)


def take_rows(row_of, table_ref, out_ref, count, group=16):
    def body(step, carry):
        base = pl.multiple_of(step * group, group)
        loaded = [table_ref[pl.ds(row_of(base + j), 1), :] for j in range(group)]
        out_ref[pl.ds(base, group), :] = jnp.concatenate(loaded, axis=0)
        return carry

    lax.fori_loop(0, count // group, body, 0)


def widen(table, start, ref):
    size = ref.shape[0]
    table[pl.ds(pl.multiple_of(start, 256), size), :] = ref[...].astype(jnp.float32)


def apply_kernel(first, counts_ref, blocks_ref, values_ref, mass_ref, *refs):
    out_ref, blocks, values, mass, sems = refs[-5:]
    count, nodes, width = values.shape
    slots = values_ref.shape[0]
    copies = [
        (
            pltpu.make_async_copy(blocks_ref.at[first + e], blocks.at[e], sems.at[0, e]),
            pltpu.make_async_copy(values_ref.at[first + e], values.at[e], sems.at[1, e]),
        )
        for e in range(count)
    ]
    weighing = pltpu.make_async_copy(mass_ref.at[pl.ds(first, count)], mass, sems.at[2, 0])
    weighing.start()
    for pair in copies:
        for copy in pair:
            copy.start()
    weighing.wait()
    live = counts_ref[0] - lax.axis_index("col") * slots - first
    for e, pair in enumerate(copies):
        for copy in pair:
            copy.wait()
        value = values[e]
        product = jnp.dot(blocks[e], value, preferred_element_type=jnp.float32)
        weights = jnp.broadcast_to(mass[e], (width, nodes)).T
        product = product + weights * value.astype(jnp.float32)
        out_ref[pl.ds(e * nodes, nodes), :] = jnp.where(e < live, product, 0.0).astype(jnp.bfloat16)


def apply_chunk(counts, stiffness, panel, mass, first, count, earlier):
    nodes, width = panel.shape[1:]
    return pl.pallas_call(
        functools.partial(apply_kernel, first),
        in_specs=[SMEM, HBM, HBM, HBM] + [ANY] * len(earlier),
        out_specs=VMEM,
        out_shape=jax.ShapeDtypeStruct((count * nodes, width), jnp.bfloat16),
        scratch_shapes=[
            pltpu.VMEM((count, nodes, nodes), jnp.bfloat16),
            pltpu.VMEM((count, nodes, width), jnp.bfloat16),
            pltpu.VMEM((count, 1, nodes), jnp.float32),
            pltpu.SemaphoreType.DMA((3, count)),
        ],
        compiler_params=params(12),
        cost_estimate=cost(2 * count * nodes * nodes * width, 2 * count * nodes * (nodes + 2 * width)),
        name="apply",
    )(counts, in_hbm(stiffness), in_hbm(panel), in_hbm(mass), *earlier)


def pick_kernel(steps, rows_ref, in_ref, prev_ref, next_ref, held, table, taken, sems):
    size = held.shape[1]
    copies = [
        pltpu.make_async_copy(in_ref.at[pl.ds(j * size, size)], held.at[j], sems.at[j]) for j in range(steps)
    ]
    for copy in copies:
        copy.start()
    for j, copy in enumerate(copies):
        copy.wait()
        widen(table, j * size, held.at[j])
    count = taken.shape[0]
    take_rows(lambda i: rows_ref[i], table, taken, count, 32)
    prev_ref[...] = taken[...].astype(jnp.bfloat16)
    take_rows(lambda i: rows_ref[count + i], table, taken, count, 32)
    next_ref[...] = taken[...].astype(jnp.bfloat16)


def pick_resident(lists, resident):
    total, width = resident.shape
    count = lists.shape[0] // 2
    steps = 8
    return pl.pallas_call(
        functools.partial(pick_kernel, steps),
        in_specs=[SMEM, HBM],
        out_specs=[VMEM] * 2,
        scratch_shapes=[
            pltpu.VMEM((steps, total // steps, width), jnp.bfloat16),
            pltpu.VMEM((total, width), jnp.float32),
            pltpu.VMEM((count, width), jnp.float32),
            pltpu.SemaphoreType.DMA((steps,)),
        ],
        out_shape=[jax.ShapeDtypeStruct((count, width), jnp.bfloat16)] * 2,
        compiler_params=params(44),
        cost_estimate=cost(0, 4 * total * width),
        name="pick_resident",
    )(lists, in_hbm(resident))


def edge_kernel(places, rows_ref, *refs):
    pieces = len(places)
    ins, (out_ref, last_ref, table, taken) = refs[:pieces], refs[-4:]
    last_ref[...] = ins[pieces // 2 - 1][...]
    span = table.shape[0] - 8
    core = lax.axis_index("col") % 2
    for (flip, offset), ref in zip(places, ins):
        widen(table, (core ^ flip) * (span // 2) + offset, ref)
    table[pl.ds(span, 8), :] = jnp.zeros((8, table.shape[1]), jnp.float32)
    take_rows(lambda i: rows_ref[i], table, taken, taken.shape[0])
    out_ref[...] = taken[...].astype(jnp.bfloat16)


def pick_edge(rows, pieces, places, span, *earlier):
    last = pieces[len(pieces) // 2 - 1]
    width = pieces[0].shape[1]
    count = rows.shape[0]
    return pl.pallas_call(
        functools.partial(edge_kernel, places),
        in_specs=[SMEM] + [VMEM] * len(pieces) + [ANY] * len(earlier),
        out_specs=[VMEM, VMEM],
        scratch_shapes=[pltpu.VMEM((span + 8, width), jnp.float32), pltpu.VMEM((count, width), jnp.float32)],
        out_shape=[jax.ShapeDtypeStruct(shape, jnp.bfloat16) for shape in ((count, width), last.shape)],
        compiler_params=params(16),
        cost_estimate=cost(0, 8 * span * width),
        name="pick_edge",
    )(rows, *pieces, *earlier)


def hold_kernel(parts, in_ref, *refs):
    size = in_ref.shape[0] // parts
    for j, out_ref in enumerate(refs[-parts:]):
        out_ref[...] = in_ref[pl.ds(j * size, size), :]


def hold(value, parts, *earlier):
    shape = (value.shape[0] // parts, value.shape[1])
    return pl.pallas_call(
        functools.partial(hold_kernel, parts),
        in_specs=[VMEM] + [ANY] * len(earlier),
        out_specs=[VMEM] * parts,
        out_shape=[jax.ShapeDtypeStruct(shape, value.dtype)] * parts,
        compiler_params=params(8),
        cost_estimate=cost(0, 4 * value.size),
        name="hold",
    )(value, *earlier)


def edge_gram_kernel(prev_ref, next_ref, mine_ref, other_ref, total_ref, out_ref):
    half = mine_ref.shape[0]
    core = lax.axis_index("col") % 2
    mine = pl.ds(pl.multiple_of(core * half, half), half)
    other = pl.ds(pl.multiple_of((1 - core) * half, half), half)
    first = lax.axis_index("row") % LINE == 0

    @pl.when(first)
    def _():
        out_ref[...] = total_ref[...] + dot0(prev_ref[mine, :], mine_ref[...]) + dot0(prev_ref[other, :], other_ref[...])

    @pl.when(jnp.logical_not(first))
    def _():
        out_ref[...] = total_ref[...] + dot0(next_ref[mine, :], mine_ref[...]) + dot0(next_ref[other, :], other_ref[...])


def edge_gram(prev_out, next_out, mine, other, total):
    arrays = (prev_out, next_out, mine, other, total)
    return pl.pallas_call(
        edge_gram_kernel,
        in_specs=[VMEM] * len(arrays),
        out_specs=VMEM,
        out_shape=jax.ShapeDtypeStruct(total.shape, jnp.float32),
        compiler_params=params(8),
        cost_estimate=cost(2 * prev_out.size * mine.shape[1], 4 * prev_out.size),
        name="edge_gram",
    )(*arrays)


def gram_steps(places, left_ref, ins, held, sems):
    slots, size = held.shape[:2]
    column = lax.axis_index("col")
    share = left_ref.shape[0] // lax.axis_size("col")
    blocks = [
        (flip, offset + start, ref, start)
        for (flip, offset), ref in zip(places, ins)
        for start in range(0, ref.shape[0], size)
    ]

    def copy(j):
        flip, offset = blocks[j][:2]
        start = pl.multiple_of((column ^ flip) * share + offset, 256)
        return pltpu.make_async_copy(left_ref.at[pl.ds(start, size)], held.at[j % slots], sems.at[j % slots])

    def begin():
        for j in range(min(slots, len(blocks))):
            copy(j).start()

    def finish(total):
        for j, (_, _, ref, start) in enumerate(blocks):
            copy(j).wait()
            product = dot0(held[j % slots], ref[pl.ds(start, size), :])
            total = product if total is None else total + product
            if j + slots < len(blocks):
                copy(j + slots).start()
        return total

    return begin, finish


def gram_kernel(places, has_total, left_ref, *refs):
    count = len(places)
    held, sems = refs[-2:]
    begin, finish = gram_steps(places, left_ref, refs[:count], held, sems)
    begin()
    refs[-3][...] = finish(refs[count][...] if has_total else None)


def gram_of(resident, pieces, places, total=None, earlier=()):
    width = pieces[0].shape[1]
    columns = resident.shape[1]
    slots, block = 4, math.gcd(*(piece.shape[0] for piece in pieces))
    height = sum(piece.shape[0] for piece in pieces)
    return pl.pallas_call(
        functools.partial(gram_kernel, places, total is not None),
        in_specs=[HBM] + [VMEM] * (len(pieces) + (total is not None)) + [ANY] * len(earlier),
        out_specs=VMEM,
        out_shape=jax.ShapeDtypeStruct((columns, width), jnp.float32),
        scratch_shapes=[
            pltpu.VMEM((slots, block, columns), jnp.bfloat16),
            pltpu.SemaphoreType.DMA((slots,)),
        ],
        compiler_params=params(16),
        cost_estimate=cost(2 * height * columns * width, 2 * height * (columns + width)),
        name="gram_of",
    )(in_hbm(resident), *pieces, *([] if total is None else [total]), *earlier)


def early_kernel(places, rows_ref, *refs):
    pieces = len(places)
    ins, out_ref, table, taken = refs[:pieces], refs[pieces], refs[pieces + 1], refs[pieces + 2]
    column = lax.axis_index("col")
    share = table.shape[0] // lax.axis_size("col")
    for (flip, offset), ref in zip(places, ins):
        widen(table, (column ^ flip) * share + offset, ref)
    size = share - ins[0].shape[0]
    for flip in (2, 3):
        late = pl.multiple_of((column ^ flip) * share + share - size, 512)
        table[pl.ds(late, size), :] = jnp.zeros((size, table.shape[1]), jnp.float32)
    take_rows(lambda i: rows_ref[i], table, taken, taken.shape[0])
    out_ref[...] = taken[...].astype(jnp.bfloat16)


def pick_early(lists, pieces, places, total):
    width = pieces[0].shape[1]
    count = lists.shape[0]
    return pl.pallas_call(
        functools.partial(early_kernel, places),
        in_specs=[SMEM] + [VMEM] * len(pieces),
        out_specs=VMEM,
        scratch_shapes=[pltpu.VMEM((total, width), jnp.float32), pltpu.VMEM((count, width), jnp.float32)],
        out_shape=jax.ShapeDtypeStruct((count, width), jnp.bfloat16),
        compiler_params=params(24),
        cost_estimate=cost(0, 4 * total * width),
        name="pick_early",
    )(lists, *pieces)


def last_kernel(rows_ref, left_ref, prev_ref, next_ref, early_ref, total_ref, far_ref, mate_ref, out_ref, held, table, taken, sems):
    size = far_ref.shape[0]
    count = prev_ref.shape[0]
    share = left_ref.shape[0] // lax.axis_size("col")
    places = ((2, share - size), (3, share - size))
    begin, finish = gram_steps(places, left_ref, (far_ref, mate_ref), held, sems)
    begin()
    table[pl.ds(0, size), :] = far_ref[...].astype(jnp.float32)
    table[pl.ds(size, size), :] = mate_ref[...].astype(jnp.float32)
    table[pl.ds(2 * size, 8), :] = jnp.zeros((8, table.shape[1]), jnp.float32)
    take_rows(lambda i: rows_ref[i], table, taken, 2 * count)
    got = early_ref[...] + taken[...].astype(jnp.bfloat16)
    total = total_ref[...] + dot0(prev_ref[...], got[:count]) + dot0(next_ref[...], got[count:])
    out_ref[...] = finish(total)


def gram_last(rows, resident, from_prev, from_next, early, total, far, mate):
    size, width = far.shape
    columns = resident.shape[1]
    count = rows.shape[0] // 2
    return pl.pallas_call(
        last_kernel,
        in_specs=[SMEM, HBM] + [VMEM] * 6,
        out_specs=VMEM,
        scratch_shapes=[
            pltpu.VMEM((2, size, columns), jnp.bfloat16),
            pltpu.VMEM((2 * size + 8, width), jnp.float32),
            pltpu.VMEM((2 * count, width), jnp.float32),
            pltpu.SemaphoreType.DMA((2,)),
        ],
        out_shape=jax.ShapeDtypeStruct((columns, width), jnp.float32),
        compiler_params=params(24),
        cost_estimate=cost(4 * (size + count) * columns * width, 8 * (size + count) * columns),
        name="gram_last",
    )(rows, in_hbm(resident), from_prev, from_next, early, total, far, mate)


def shards(panel, stiffness, mass, resident, face_rows, counts):
    slots, nodes, width = panel.shape[1:]
    cols, rows = lax.axis_size("col"), lax.axis_size("row")
    resident = resident[0]
    columns = resident.shape[1]
    weights = mass[0].reshape(slots, 1, nodes)

    def permute(value, move):
        pairs = []
        for source in range(cols * rows):
            target = move(*divmod(source, rows))
            if target is not None:
                pairs.append((source, target[0] * rows + target[1]))
        return lax.ppermute(value, AXES, pairs)

    def across(value):
        return permute(value, lambda c, r: (c ^ 2, r))

    def sibling(value):
        return permute(value, lambda c, r: (c ^ 1, r))

    column, row = lax.axis_index("col"), lax.axis_index("row")
    share = slots * nodes
    per = slots // sum(SPLIT)
    pieces, offsets = [], []
    for k, parts in enumerate(SPLIT):
        first = per * sum(SPLIT[:k])
        pieces.append(apply_chunk(counts, stiffness[0], panel[0], weights, first, per * parts, pieces[-1:]))
        offsets.append(first * nodes)
    far = [across(piece) for piece in pieces[:-1]]
    mate = [sibling(piece) for piece in pieces]
    here = [(flip, offset) for flip in (0, 1) for offset in offsets]

    lists = face_rows[0].reshape(-1)
    count = face_rows.shape[2]
    prev_out, next_out = pick_resident(lists, resident)
    from_prev = permute(next_out, lambda c, r: (c, r + 1) if r % LINE != LINE - 1 else None)
    from_next = permute(prev_out, lambda c, r: (c, r - 1) if r % LINE != 0 else None)

    edge_rows = jnp.where(row % LINE == 0, lists[:count], lists[count:])
    half = count // 2
    edge_rows = jnp.where(column % 2 == 0, edge_rows[:half], edge_rows[half:]) - column // 2 * 2 * share
    edge_rows = jnp.where((edge_rows >= 0) & (edge_rows < 2 * share), edge_rows, 2 * share)
    edge, last = pick_edge(edge_rows, pieces + mate, here, 2 * share, prev_out)
    far.append(across(last))

    def beside(c, r):
        if r % LINE == LINE - 1 and r + 1 < rows:
            return c, r + 1
        if r % LINE == 0 and r > 0:
            return c, r - 1
        return None

    def crossed(c, r):
        target = beside(c, r)
        return target if target is None else (target[0] ^ 2, target[1])

    near_half, far_half = permute(edge, beside), permute(edge, crossed)
    met = near_half + far_half
    other = sibling(met)
    parts = 2
    far_mate = [sibling(part) for part in hold(far[0], parts, edge)]
    height = offsets[1] // parts
    arrived = [far[0]] + far_mate
    there = [(2, 0)] + [(3, j * height) for j in range(parts)]
    early = pick_early(lists, pieces + mate + arrived, here + there, resident.shape[0])
    total = gram_of(resident, pieces + mate, here)
    total = gram_of(resident, arrived, there, total, (from_prev, from_next))
    last_mate = sibling(hold(far[1], 1, early, total)[0])
    total = edge_gram(prev_out, next_out, met, other, total)
    size = far[-1].shape[0]
    late_rows = jnp.full_like(lists, 2 * size)
    for j, flip in enumerate((2, 3)):
        found = lists - ((column ^ flip) * share + share - size)
        late_rows = jnp.where((found >= 0) & (found < size), found + j * size, late_rows)
    gram = gram_last(late_rows, resident, from_prev, from_next, early, total, far[-1], last_mate)

    own_rows = columns // rows
    received = lax.all_to_all(gram.reshape(rows, own_rows, width), "row", 0, 0)
    return jnp.sum(received, axis=0)


def solution(mesh):
    in_specs = (
        P("row", "col", None, None),
        P("row", "col", None, None),
        P("row", "col", None),
        P("row", None, "col"),
        P("row", None, None),
        P("row"),
    )
    out_specs = P(("col", "row"), None)
    return jax.shard_map(shards, mesh=mesh, in_specs=in_specs, out_specs=out_specs, check_vma=False)
```

time: 439 us -> 94.6 us (0.22)
  waiting for transfers between devices: 333 us -> 4.72 us
  Pallas kernels: 0 us -> 51.8 us
  other arithmetic: 46.4 us -> 1.53 us
  blocking collectives: 0 us -> 21.1 us
  local copies, waits for them, and re-layouts: 20.7 us -> 0.65 us
  matrix products: 17.5 us -> 0 us
  between operations: 14.1 us -> 0.96 us
  starting transfers between devices: 5.91 us -> 13.4 us
    psum x1 -> x0, waiting for transfers between devices: 281 us -> none  [shards(): full_gram = lax.psum(partial_gram, 'row')]
    all_gather x1 -> x0, waiting for transfers between devices: 52.9 us -> none  [shards(): whole = lax.all_gather(local_rows, 'col', axis=0, tiled=True)]
    pallas_call x0 -> x11, Pallas kernels: none -> 51.8 us  [the longest x1 15.3 us: pick_resident(): pl.pallas_call(functools.partial(pick_kernel, steps), in_specs=[SMEM, HBM...]
    scatter-add x2 -> x0, other arithmetic: 39 us -> none  [the longest x1 19.5 us: shards(): summed = summed.at[prev_rows].add(from_prev.astype(jnp.float32))]
    all_to_all x0 -> x1, blocking collectives: none -> 21.1 us  [shards(): received = lax.all_to_all(gram.reshape(rows, own_rows, width), 'row', 0, 0)]
    gather x2 -> x0, local copies, waits for them, and re-layouts: 18.4 us -> none  [the longest x1 9.19 us: shards(): from_prev = passed_along(whole[next_rows], 'row', 1)]
    dot_general x2 -> x0, matrix products: 17.5 us -> none  [the longest x1 10.8 us: shards(): lax.dot_general(columns, summed, contract, preferred_element_type=jnp.flo...]
    ppermute x2 -> x12, starting transfers between devices: 5.87 us -> 13.4 us  [permute(): return lax.ppermute(value, AXES, pairs)]
  transfers between devices with their start and end apart: 4 -> 12, of which waited for: 2 -> 5; matrix products, arithmetic and copies ran while one was open for 8% -> 1% of each run, Pallas kernels for 0% -> 41%
where the time goes in v3:
time: 94.6 us; the launch traced here: 94.2 us
  Pallas kernels  51.8 us (55%)
  blocking collectives  21.1 us (22%)
  starting transfers between devices  13.4 us (14%)
  waiting for transfers between devices  4.72 us (5%)
  other arithmetic  1.53 us (2%)
  between operations  0.96 us (1%)
    all_to_all x1, blocking collectives, shards(): received = lax.all_to_all(gram.reshape(rows, own_rows, width), 'row', 0, 0)  21.1 us
    pallas_call x1, Pallas kernels, pick_resident(): pl.pallas_call(functools.partial(pick_kernel, steps), in_specs=[SMEM, HBM...  15.3 us
    ppermute x12, starting transfers between devices, permute(): return lax.ppermute(value, AXES, pairs)  13.4 us
    pallas_call x2, Pallas kernels, gram_of(): pl.pallas_call(functools.partial(gram_kernel, places, total is not None),...  9.04 us
    pallas_call x2, Pallas kernels, apply_chunk(): pl.pallas_call(functools.partial(apply_kernel, first), in_specs=[SMEM, HB...  8.09 us
    pallas_call x1, Pallas kernels, gram_last(): pl.pallas_call(last_kernel, in_specs=[SMEM, HBM] + [VMEM] * 6, out_specs=...  7.84 us
    pallas_call x1, Pallas kernels, pick_early(): pl.pallas_call(functools.partial(early_kernel, places), in_specs=[SMEM] +...  6.63 us
    ppermute x12, waiting for transfers between devices, permute(): return lax.ppermute(value, AXES, pairs)  4.72 us
  transfers between devices with their start and end apart: 12, of which 5 were waited for; matrix products, arithmetic and copies ran while one was open for 1% of the time, Pallas kernels for 41%

profile of v3, /device:TPU:0, one launch (start us, length us, event | category | flops | bytes accessed | tf_op | source)
XLA Modules:
  0.0 94.2 jit_solution(15284178450852134147)
XLA Ops:
  0.7 5.0 %apply.2.refs_0_ = bf16[4608,128]{1,0:T(8,128)(2,1)S(1)} custom-call(s32[1]{0:T(128)S(6)} %copy.8.counts_ref, bf16[12,512,512]{2,1,0:T(8,128)(2,1)} %bitcast.16, bf16[12,512,128]{2,1,0:T(8,128)(2,1)} %bitcast.18, f32[12,1,512]{2,1,0:T(1,128)} %bitcast.20), custom_call_target="tpu_custom_call" | custom-call | flops 603979776 | bytes 7077888 | tf_op jit(solution)/shard_map/apply/pallas_call | solution.py:85
  5.7 0.0 copy-start.4
  5.7 0.1 collective-permute-start.2
  5.8 3.4 %collective-permute-start.4 = (bf16[4608,128]{1,0:T(8,128)(2,1)S(1)}, bf16[4608,128]{1,0:T(8,128)(2,1)S(1)}, u32[]{:S(2)}, u32[]{:S(2)}) collective-permute-start(bf16[4608,128]{1,0:T(8,128)(2,1)S(1)} %apply.2.refs_0_), channel_id=1, source_target_pairs={{0,64},{1,65},{2,66},{3,67},{4,68},{5,69},{6,70},{7,71},{8,72},{9,... | collective-permute-start | bytes 3538952 | tf_op jit(solution)/shard_map/ppermute | solution.py:356
  9.1 3.1 %apply.3.refs_1_ = bf16[1536,128]{1,0:T(8,128)(2,1)} custom-call(s32[1]{0:T(128)S(6)} %copy.8.counts_ref, bf16[12,512,512]{2,1,0:T(8,128)(2,1)} %bitcast.17, bf16[12,512,128]{2,1,0:T(8,128)(2,1)} %bitcast.19, f32[12,1,512]{2,1,0:T(1,128)} %bitcast.21, bf16[4608,128]{1,0:T(8,128)(2,1)S(1)} %apply.2.refs_0_), custom_call_target="tpu_custom_call" | custom-call | flops 201326592 | bytes 2359296 | tf_op jit(solution)/shard_map/apply/pallas_call | solution.py:85
  12.2 0.2 collective-permute-start.3
  12.5 0.0 copy-done.4
  12.5 15.3 %pick_resident.1 = (bf16[2048,256]{1,0:T(8,128)(2,1)}, bf16[2048,256]{1,0:T(8,128)(2,1)}) custom-call(s32[4096]{0:T(1024)S(1)} %bitcast.9, bf16[24576,256]{1,0:T(8,128)(2,1)} %bitcast.12), custom_call_target="tpu_custom_call" | custom-call | bytes 25165824 | tf_op jit(solution)/shard_map/pick_resident/pallas_call | solution.py:123
  27.8 1.3 %collective-permute-start.1 = (bf16[2048,256]{1,0:T(8,128)(2,1)}, bf16[2048,256]{1,0:T(8,128)(2,1)}, u32[]{:S(2)}, u32[]{:S(2)}) collective-permute-start(bf16[2048,256]{1,0:T(8,128)(2,1)} %get-tuple-element.12.refs_4_.prev_ref), channel_id=1, source_target_pairs={{1,0},{2,1},{3,2},{5,4},{6,5},{7,6},{9,8},{10,9},{11,10},{13,12},{... | collective-permute-start | bytes 3145736 | tf_op jit(solution)/shard_map/ppermute | solution.py:356
  29.1 5.5 %collective-permute-start = (bf16[2048,256]{1,0:T(8,128)(2,1)}, bf16[2048,256]{1,0:T(8,128)(2,1)}, u32[]{:S(2)}, u32[]{:S(2)}) collective-permute-start(bf16[2048,256]{1,0:T(8,128)(2,1)} %get-tuple-element.11.next_ref), channel_id=1, source_target_pairs={{0,1},{1,2},{2,3},{4,5},{5,6},{6,7},{8,9},{9,10},{10,11},{12,13},{... | collective-permute-start | bytes 3145736 | tf_op jit(solution)/shard_map/ppermute | solution.py:356
  34.7 0.8 broadcast_select_fusion
  35.5 0.0 collective-permute-done.3.refs_3_
  35.5 0.0 collective-permute-done.2.refs_2_
  35.5 2.7 %pick_edge.1 = (bf16[1024,128]{1,0:T(8,128)(2,1)S(1)}, bf16[1536,128]{1,0:T(8,128)(2,1)S(1)}) custom-call(s32[1024]{0:T(1024)S(1)} %and_select_fusion.rows_ref, bf16[4608,128]{1,0:T(8,128)(2,1)S(1)} %apply.2.refs_0_, bf16[1536,128]{1,0:T(8,128)(2,1)} %apply.3.refs_1_, bf16[4608,128]{1,0:T(8,128)(2,1)S(1)} %collective-permute-done.2.refs_2_, ...), custom_call_target="tpu_custom_call" | custom-call | bytes 12582912 | tf_op jit(solution)/shard_map/pick_edge/pallas_call | solution.py:157
  38.3 0.0 collective-permute-done.4.in_ref.refs_4_.refs_0_
  38.3 0.1 hold.2
  38.4 0.1 collective-permute-start.5
  38.5 0.5 collective-permute-start.6
  39.0 0.7 collective-permute-start.10
  39.6 0.8 collective-permute-done.5.refs_5_.refs_1_
  40.5 0.7 collective-permute-start.7
  41.1 0.2 collective-permute-done.6.refs_6_.refs_2_
  41.3 0.8 collective-permute-start.8
  42.1 5.6 %gram_of.2.refs_3_ = f32[256,128]{1,0:T(8,128)S(1)} custom-call(bf16[24576,256]{1,0:T(8,128)(2,1)} %bitcast.13, bf16[4608,128]{1,0:T(8,128)(2,1)S(1)} %apply.2.refs_0_, bf16[1536,128]{1,0:T(8,128)(2,1)} %apply.3.refs_1_, bf16[4608,128]{1,0:T(8,128)(2,1)S(1)} %collective-permute-done.2.refs_2_, bf16[1536,128]{1,0:T(8,128)(2,1)} %collective-permute-done.3.refs_3_), custom_call_target="tpu_custom_call" | custom-call | flops 805306368 | bytes 9437184 | tf_op jit(solution)/shard_map/gram_of/pallas_call | solution.py:261
  47.8 6.6 %pick_early.1.refs_0_.early_ref = bf16[4096,128]{1,0:T(8,128)(2,1)S(1)} custom-call(s32[4096]{0:T(1024)S(1)} %bitcast.10, bf16[4608,128]{1,0:T(8,128)(2,1)S(1)} %apply.2.refs_0_, bf16[1536,128]{1,0:T(8,128)(2,1)} %apply.3.refs_1_, bf16[4608,128]{1,0:T(8,128)(2,1)S(1)} %collective-permute-done.2.refs_2_, bf16[1536,128]{1,0:T(8,128)(2,1)} %collective-permute-done.3.refs_3_, ...), custom_call_target="tpu_custom_call" | custom-call | bytes 12582912 | tf_op jit(solution)/shard_map/pick_early/pallas_call | solution.py:294
  54.4 0.0 copy-start
  54.4 1.0 %collective-permute-done.1.refs_5_.next_ref = bf16[2048,256]{1,0:T(8,128)(2,1)} collective-permute-done((bf16[2048,256]{1,0:T(8,128)(2,1)}, bf16[2048,256]{1,0:T(8,128)(2,1)}, u32[]{:S(2)}, u32[]{:S(2)}) %collective-permute-start.1) | collective-permute-done | bytes 1048608 | tf_op jit(solution)/shard_map/ppermute | solution.py:356
  55.4 1.2 %collective-permute-done.refs_4_.prev_ref = bf16[2048,256]{1,0:T(8,128)(2,1)} collective-permute-done((bf16[2048,256]{1,0:T(8,128)(2,1)}, bf16[2048,256]{1,0:T(8,128)(2,1)}, u32[]{:S(2)}, u32[]{:S(2)}) %collective-permute-start) | collective-permute-done | bytes 1048608 | tf_op jit(solution)/shard_map/ppermute | solution.py:356
  56.6 3.4 %gram_of.3.total_ref.refs_1_ = f32[256,128]{1,0:T(8,128)S(1)} custom-call(bf16[24576,256]{1,0:T(8,128)(2,1)} %bitcast.14, bf16[4608,128]{1,0:T(8,128)(2,1)S(1)} %collective-permute-done.4.in_ref.refs_4_.refs_0_, bf16[2304,128]{1,0:T(8,128)(2,1)S(1)} %collective-permute-done.5.refs_5_.refs_1_, bf16[2304,128]{1,0:T(8,128)(2,1)S(1)} %collective-permute-done.6.refs_6_.refs_2_, ...), custom_call_target="tpu_custom_call" | custom-call | flops 603979776 | bytes 7077888 | tf_op jit(solution)/shard_map/gram_of/pallas_call | solution.py:261
  60.1 0.0 collective-permute-done.10.in_ref.far_ref
  60.1 0.0 copy-done
  60.1 0.0 copy-start.2
  60.1 0.1 collective-permute-start.11
  60.2 0.0 collective-permute-done.7
  60.2 0.0 collective-permute-done.8
  60.2 0.6 copy-done.2
  60.9 0.1 add.25.mine_ref
  60.9 0.0 copy-start.1
  61.0 0.0 copy-start.3
  61.0 0.1 collective-permute-start.9
  61.1 1.5 %collective-permute-done.9.other_ref = bf16[1024,128]{1,0:T(8,128)(2,1)S(1)} collective-permute-done((bf16[1024,128]{1,0:T(8,128)(2,1)S(1)}, bf16[1024,128]{1,0:T(8,128)(2,1)S(1)}, u32[]{:S(2)}, u32[]{:S(2)}) %collective-permute-start.9) | collective-permute-done | bytes 262176 | tf_op jit(solution)/shard_map/ppermute | solution.py:356
  62.6 2.0 %edge_gram.1.total_ref = f32[256,128]{1,0:T(8,128)S(1)} custom-call(bf16[2048,256]{1,0:T(8,128)(2,1)} %get-tuple-element.12.refs_4_.prev_ref, bf16[2048,256]{1,0:T(8,128)(2,1)} %get-tuple-element.11.next_ref, bf16[1024,128]{1,0:T(8,128)(2,1)S(1)} %add.25.mine_ref, bf16[1024,128]{1,0:T(8,128)(2,1)S(1)} %collective-permute-done.9.other_ref, ...), custom_call_target="tpu_custom_call" | custom-call | flops 134217728 | bytes 2097152 | tf_op jit(solution)/shard_map/edge_gram/pallas_call | solution.py:206
  64.6 0.0 collective-permute-done.11.mate_ref
  64.6 0.0 copy-done.1
  64.6 0.0 copy-done.3
  64.6 7.8 %gram_last.1 = f32[256,128]{1,0:T(8,128)S(1)} custom-call(s32[4096]{0:T(1024)S(1)} %select_select_fusion.rows_ref, bf16[24576,256]{1,0:T(8,128)(2,1)} %bitcast.15, bf16[2048,256]{1,0:T(8,128)(2,1)} %collective-permute-done.refs_4_.prev_ref, bf16[2048,256]{1,0:T(8,128)(2,1)} %collective-permute-done.1.refs_5_.next_ref, bf16[4096,128]{1,0:T(8,128)(2,1)S(1)} %copy-done.1, ...), custom_call_target="tpu_custom_call" | custom-call | flops 469762048 | bytes 7340032 | tf_op jit(solution)/shard_map/gram_last/pallas_call | solution.py:326
  72.5 21.1 %all_to_all.5 = f32[32,8,128]{2,1,0:T(8,128)S(1)} all-to-all(f32[32,8,128]{2,1,0:T(8,128)S(1)} %bitcast.8), channel_id=1, replica_groups=mesh['col'=4,'row'=32] {'row'}, dimensions={0} | all-to-all | bytes 262144 | tf_op jit(solution)/shard_map/all_to_all | solution.py:421
  93.6 0.6 reduce_sum.9
  (5 shorter events, 0.1 us)
Async XLA Ops:
  5.7 6.8 %copy-start.4 = (s32[1,2,2048]{2,1,0:T(2,128)S(1)}, s32[1,2,2048]{2,1,0:T(2,128)}, u32[]{:S(2)}) copy-start(s32[1,2,2048]{2,1,0:T(2,128)} %param.10) | copy-start | bytes 49156
  5.7 29.8 %collective-permute-start.2 = (bf16[4608,128]{1,0:T(8,128)(2,1)S(1)}, bf16[4608,128]{1,0:T(8,128)(2,1)S(1)}, u32[]{:S(2)}, u32[]{:S(2)}) collective-permute-start(bf16[4608,128]{1,0:T(8,128)(2,1)S(1)} %apply.2.refs_0_), channel_id=1, source_target_pairs={{0,32},{1,33},{2,34},{3,35},{4,36},{5,37},{6,38},{7,39},{8,40},{9,... | collective-permute-start | bytes 3538952 | tf_op jit(solution)/shard_map/ppermute | solution.py:356
  5.8 32.5 %collective-permute-start.4 = (bf16[4608,128]{1,0:T(8,128)(2,1)S(1)}, bf16[4608,128]{1,0:T(8,128)(2,1)S(1)}, u32[]{:S(2)}, u32[]{:S(2)}) collective-permute-start(bf16[4608,128]{1,0:T(8,128)(2,1)S(1)} %apply.2.refs_0_), channel_id=1, source_target_pairs={{0,64},{1,65},{2,66},{3,67},{4,68},{5,69},{6,70},{7,71},{8,72},{9,... | collective-permute-start | bytes 3538952 | tf_op jit(solution)/shard_map/ppermute | solution.py:356
  12.2 23.3 %collective-permute-start.3 = (bf16[1536,128]{1,0:T(8,128)(2,1)}, bf16[1536,128]{1,0:T(8,128)(2,1)}, u32[]{:S(2)}, u32[]{:S(2)}) collective-permute-start(bf16[1536,128]{1,0:T(8,128)(2,1)} %apply.3.refs_1_), channel_id=1, source_target_pairs={{0,32},{1,33},{2,34},{3,35},{4,36},{5,37},{6,38},{7,39},{8,40},{9,... | collective-permute-start | bytes 1179656 | tf_op jit(solution)/shard_map/ppermute | solution.py:356
  27.8 27.6 %collective-permute-start.1 = (bf16[2048,256]{1,0:T(8,128)(2,1)}, bf16[2048,256]{1,0:T(8,128)(2,1)}, u32[]{:S(2)}, u32[]{:S(2)}) collective-permute-start(bf16[2048,256]{1,0:T(8,128)(2,1)} %get-tuple-element.12.refs_4_.prev_ref), channel_id=1, source_target_pairs={{1,0},{2,1},{3,2},{5,4},{6,5},{7,6},{9,8},{10,9},{11,10},{13,12},{... | collective-permute-start | bytes 3145736 | tf_op jit(solution)/shard_map/ppermute | solution.py:356
  29.1 27.5 %collective-permute-start = (bf16[2048,256]{1,0:T(8,128)(2,1)}, bf16[2048,256]{1,0:T(8,128)(2,1)}, u32[]{:S(2)}, u32[]{:S(2)}) collective-permute-start(bf16[2048,256]{1,0:T(8,128)(2,1)} %get-tuple-element.11.next_ref), channel_id=1, source_target_pairs={{0,1},{1,2},{2,3},{4,5},{5,6},{6,7},{8,9},{9,10},{10,11},{12,13},{... | collective-permute-start | bytes 3145736 | tf_op jit(solution)/shard_map/ppermute | solution.py:356
  38.4 2.1 %collective-permute-start.5 = (bf16[2304,128]{1,0:T(8,128)(2,1)S(1)}, bf16[2304,128]{1,0:T(8,128)(2,1)S(1)}, u32[]{:S(2)}, u32[]{:S(2)}) collective-permute-start(bf16[2304,128]{1,0:T(8,128)(2,1)S(1)} %get-tuple-element.14), channel_id=1, source_target_pairs={{0,32},{1,33},{2,34},{3,35},{4,36},{5,37},{6,38},{7,39},{8,40},{9,... | collective-permute-start | bytes 1769480 | tf_op jit(solution)/shard_map/ppermute | solution.py:356
  38.5 2.8 %collective-permute-start.6 = (bf16[2304,128]{1,0:T(8,128)(2,1)S(1)}, bf16[2304,128]{1,0:T(8,128)(2,1)S(1)}, u32[]{:S(2)}, u32[]{:S(2)}) collective-permute-start(bf16[2304,128]{1,0:T(8,128)(2,1)S(1)} %get-tuple-element.15), channel_id=1, source_target_pairs={{0,32},{1,33},{2,34},{3,35},{4,36},{5,37},{6,38},{7,39},{8,40},{9,... | collective-permute-start | bytes 1769480 | tf_op jit(solution)/shard_map/ppermute | solution.py:356
  39.0 21.1 %collective-permute-start.10 = (bf16[1536,128]{1,0:T(8,128)(2,1)S(1)}, bf16[1536,128]{1,0:T(8,128)(2,1)S(1)}, u32[]{:S(2)}, u32[]{:S(2)}) collective-permute-start(bf16[1536,128]{1,0:T(8,128)(2,1)S(1)} %get-tuple-element.16), channel_id=1, source_target_pairs={{0,64},{1,65},{2,66},{3,67},{4,68},{5,69},{6,70},{7,71},{8,72},{9,... | collective-permute-start | bytes 1179656 | tf_op jit(solution)/shard_map/ppermute | solution.py:356
  40.5 19.8 %collective-permute-start.7 = (bf16[1024,128]{1,0:T(8,128)(2,1)S(1)}, bf16[1024,128]{1,0:T(8,128)(2,1)S(1)}, u32[]{:S(2)}, u32[]{:S(2)}) collective-permute-start(bf16[1024,128]{1,0:T(8,128)(2,1)S(1)} %get-tuple-element.13.refs_0_), channel_id=1, source_target_pairs={{3,4},{4,3},{7,8},{8,7},{11,12},{12,11},{15,16},{16,15},{19,20},{2... | collective-permute-start | bytes 786440 | tf_op jit(solution)/shard_map/ppermute | solution.py:356
  41.3 18.9 %collective-permute-start.8 = (bf16[1024,128]{1,0:T(8,128)(2,1)S(1)}, bf16[1024,128]{1,0:T(8,128)(2,1)S(1)}, u32[]{:S(2)}, u32[]{:S(2)}) collective-permute-start(bf16[1024,128]{1,0:T(8,128)(2,1)S(1)} %get-tuple-element.13.refs_0_), channel_id=1, source_target_pairs={{3,68},{4,67},{7,72},{8,71},{11,76},{12,75},{15,80},{16,79},{19,84... | collective-permute-start | bytes 786440 | tf_op jit(solution)/shard_map/ppermute | solution.py:356
  54.4 5.7 %copy-start = (bf16[4096,128]{1,0:T(8,128)(2,1)}, bf16[4096,128]{1,0:T(8,128)(2,1)S(1)}, u32[]{:S(2)}) copy-start(bf16[4096,128]{1,0:T(8,128)(2,1)S(1)} %pick_early.1.refs_0_.early_ref) | copy-start | bytes 3145732
  60.1 0.8 copy-start.2
  60.1 4.5 %collective-permute-start.11 = (bf16[1536,128]{1,0:T(8,128)(2,1)S(1)}, bf16[1536,128]{1,0:T(8,128)(2,1)S(1)}, u32[]{:S(2)}, u32[]{:S(2)}) collective-permute-start(bf16[1536,128]{1,0:T(8,128)(2,1)S(1)} %hold.3), channel_id=1, source_target_pairs={{0,32},{1,33},{2,34},{3,35},{4,36},{5,37},{6,38},{7,39},{8,40},{9,... | collective-permute-start | bytes 1179656 | tf_op jit(solution)/shard_map/ppermute | solution.py:356
  60.9 3.7 %copy-start.1 = (bf16[4096,128]{1,0:T(8,128)(2,1)S(1)}, bf16[4096,128]{1,0:T(8,128)(2,1)}, u32[]{:S(2)}) copy-start(bf16[4096,128]{1,0:T(8,128)(2,1)} %copy-done) | copy-start | bytes 3145732
  61.0 3.7 %copy-start.3 = (bf16[1536,128]{1,0:T(8,128)(2,1)S(1)}, bf16[1536,128]{1,0:T(8,128)(2,1)}, u32[]{:S(2)}) copy-start(bf16[1536,128]{1,0:T(8,128)(2,1)} %copy-done.2) | copy-start | bytes 1179652
  61.0 1.6 %collective-permute-start.9 = (bf16[1024,128]{1,0:T(8,128)(2,1)S(1)}, bf16[1024,128]{1,0:T(8,128)(2,1)S(1)}, u32[]{:S(2)}, u32[]{:S(2)}) collective-permute-start(bf16[1024,128]{1,0:T(8,128)(2,1)S(1)} %add.25.mine_ref), channel_id=1, source_target_pairs={{0,32},{1,33},{2,34},{3,35},{4,36},{5,37},{6,38},{7,39},{8,40},{9,... | collective-permute-start | bytes 786440 | tf_op jit(solution)/shard_map/ppermute | solution.py:356

commit v4 on v0

v4 whole, which is shorter than its diff:
```python
import functools
import math

import jax
import jax.numpy as jnp
from jax import lax
from jax.experimental import pallas as pl
from jax.experimental.pallas import tpu as pltpu
from jax.sharding import PartitionSpec as P

SPLIT = (1, 3)
MIB = 1024 * 1024
ROWS0 = (((0,), (0,)), ((), ()))
AXES = ("col", "row")


def params(mib):
    return pltpu.CompilerParams(vmem_limit_bytes=mib * MIB)


HBM = pl.BlockSpec(memory_space=pltpu.HBM)
ANY = pl.BlockSpec(memory_space=pl.ANY)
SMEM = pl.BlockSpec(memory_space=pltpu.SMEM)
VMEM = pl.BlockSpec(memory_space=pltpu.VMEM)


def cost(flops, moved):
    return pl.CostEstimate(flops=flops, bytes_accessed=moved, transcendentals=0)


def in_hbm(value):
    return pltpu.with_memory_space_constraint(value, pltpu.HBM)


def dot0(left, right):
    return lax.dot_general(left, right, ROWS0, preferred_element_type=jnp.float32)


def take_rows(row_of, table_ref, out_ref, start, count, group=32):
    def body(step, carry):
        base = pl.multiple_of(step * group, group)
        loaded = [table_ref[pl.ds(row_of(base + j), 1), :] for j in range(group)]
        out_ref[pl.ds(start + base, group), :] = jnp.concatenate(loaded, axis=0)
        return carry

    lax.fori_loop(0, count // group, body, 0)


def widen(table, start, ref):
    size = ref.shape[0]
    table[pl.ds(pl.multiple_of(start, 256), size), :] = ref[...].astype(jnp.float32)


def apply_steps(first, counts_ref, blocks_ref, values_ref, mass_ref, out_ref, blocks, values, mass, sems):
    count, nodes, width = values.shape
    slots = values_ref.shape[0]
    copies = [
        (
            pltpu.make_async_copy(blocks_ref.at[first + e], blocks.at[e], sems.at[0, e]),
            pltpu.make_async_copy(values_ref.at[first + e], values.at[e], sems.at[1, e]),
        )
        for e in range(count)
    ]
    weighing = pltpu.make_async_copy(mass_ref.at[pl.ds(first, count)], mass, sems.at[2, 0])

    def begin():
        weighing.start()
        for pair in copies:
            for copy in pair:
                copy.start()

    def finish():
        weighing.wait()
        live = counts_ref[0] - lax.axis_index("col") * slots - first
        for e, pair in enumerate(copies):
            for copy in pair:
                copy.wait()
            value = values[e]
            product = jnp.dot(blocks[e], value, preferred_element_type=jnp.float32)
            weights = jnp.broadcast_to(mass[e], (width, nodes)).T
            product = product + weights * value.astype(jnp.float32)
            out_ref[pl.ds(e * nodes, nodes), :] = jnp.where(e < live, product, 0.0).astype(jnp.bfloat16)

    return begin, finish


def apply_scratch(count, nodes, width):
    return [
        pltpu.VMEM((count, nodes, nodes), jnp.bfloat16),
        pltpu.VMEM((count, nodes, width), jnp.bfloat16),
        pltpu.VMEM((count, 1, nodes), jnp.float32),
        pltpu.SemaphoreType.DMA((3, count)),
    ]


def apply_kernel(first, *refs):
    begin, finish = apply_steps(first, *refs[:4], *refs[-5:])
    begin()
    finish()


def apply_chunk(counts, stiffness, panel, mass, first, count, earlier):
    nodes, width = panel.shape[1:]
    return pl.pallas_call(
        functools.partial(apply_kernel, first),
        in_specs=[SMEM, HBM, HBM, HBM] + [ANY] * len(earlier),
        out_specs=VMEM,
        out_shape=jax.ShapeDtypeStruct((count * nodes, width), jnp.bfloat16),
        scratch_shapes=apply_scratch(count, nodes, width),
        compiler_params=params(12),
        cost_estimate=cost(2 * count * nodes * nodes * width, 2 * count * nodes * (nodes + 2 * width)),
        name="apply",
    )(counts, in_hbm(stiffness), in_hbm(panel), in_hbm(mass), *earlier)


def list_starts(count):
    start = jnp.where(lax.axis_index("row") % 2 == 0, count, 0)
    return start, count - start


def pick_kernel(pieces, rows_ref, in_ref, *refs):
    first_ref, second_ref, low_ref, high_ref, again_ref, held, left, right, left_taken, right_taken, sems = refs[-11:]
    steps, size = held.shape[:2]
    copies = [
        pltpu.make_async_copy(in_ref.at[pl.ds(j * size, size)], held.at[j], sems.at[j]) for j in range(steps)
    ]
    for copy in copies:
        copy.start()
    values = jnp.concatenate([piece[...] for piece in refs[:pieces]], axis=0)
    low_ref[...] = values[: low_ref.shape[0]]
    high_ref[...] = values[low_ref.shape[0] :]
    again_ref[...] = refs[pieces][...]
    lanes = left.shape[1]
    for j, copy in enumerate(copies):
        copy.wait()
        left[pl.ds(j * size, size), :] = held[j, :, :lanes].astype(jnp.float32)
        right[pl.ds(j * size, size), :] = held[j, :, lanes:].astype(jnp.float32)
    count = left_taken.shape[0]
    group = 32
    for begins, out_ref in zip(list_starts(count), (first_ref, second_ref)):

        def body(step, carry):
            base = pl.multiple_of(step * group, group)
            rows = [rows_ref[begins + base + i] for i in range(group)]
            for table, taken in ((left, left_taken), (right, right_taken)):
                taken[pl.ds(base, group), :] = jnp.concatenate([table[pl.ds(row, 1), :] for row in rows], axis=0)
            return carry

        lax.fori_loop(0, count // group, body, 0)
        out_ref[:, :lanes] = left_taken[...].astype(jnp.bfloat16)
        out_ref[:, lanes:] = right_taken[...].astype(jnp.bfloat16)


def pick_resident(lists, resident, pieces, arrived):
    total, columns = resident.shape
    count = lists.shape[0] // 2
    steps, lanes = 8, columns // 2
    height, width = sum(piece.shape[0] for piece in pieces), pieces[0].shape[1]
    return pl.pallas_call(
        functools.partial(pick_kernel, len(pieces)),
        in_specs=[SMEM, HBM] + [VMEM] * (len(pieces) + 1),
        out_specs=[VMEM] * 5,
        scratch_shapes=[
            pltpu.VMEM((steps, total // steps, columns), jnp.bfloat16),
            pltpu.VMEM((total, lanes), jnp.float32),
            pltpu.VMEM((total, lanes), jnp.float32),
            pltpu.VMEM((count, lanes), jnp.float32),
            pltpu.VMEM((count, lanes), jnp.float32),
            pltpu.SemaphoreType.DMA((steps,)),
        ],
        out_shape=[jax.ShapeDtypeStruct((count, columns), jnp.bfloat16)] * 2
        + [jax.ShapeDtypeStruct((height // 2, width), jnp.bfloat16)] * 2
        + [jax.ShapeDtypeStruct(arrived.shape, jnp.bfloat16)],
        compiler_params=params(46),
        cost_estimate=cost(0, 4 * total * columns),
        name="pick_resident",
    )(lists, in_hbm(resident), *pieces, arrived)


def hold_kernel(parts, *refs):
    outs = list(refs[-sum(parts) :])
    for in_ref, count in zip(refs, parts):
        size = in_ref.shape[0] // count
        for j in range(count):
            outs.pop(0)[...] = in_ref[pl.ds(j * size, size), :]


def hold(values, parts, *earlier):
    shapes = [(value.shape[0] // count, value.shape[1]) for value, count in zip(values, parts) for _ in range(count)]
    return pl.pallas_call(
        functools.partial(hold_kernel, parts),
        in_specs=[VMEM] * len(values) + [ANY] * len(earlier),
        out_specs=[VMEM] * len(shapes),
        out_shape=[jax.ShapeDtypeStruct(shape, jnp.bfloat16) for shape in shapes],
        compiler_params=params(12),
        cost_estimate=cost(0, 4 * values[0].size),
        name="hold",
    )(*values, *earlier)


def join_kernel(first_ref, second_ref, _, out_ref):
    size = first_ref.shape[0]
    out_ref[pl.ds(0, size), :] = first_ref[...]
    out_ref[pl.ds(size, size), :] = second_ref[...]


def join(first, second, earlier):
    shape = (2 * first.shape[0], first.shape[1])
    return pl.pallas_call(
        join_kernel,
        in_specs=[VMEM, VMEM, ANY],
        out_specs=VMEM,
        out_shape=jax.ShapeDtypeStruct(shape, first.dtype),
        compiler_params=params(8),
        cost_estimate=cost(0, 8 * first.size),
        name="join",
    )(first, second, earlier)


def gram_steps(places, left_ref, ins, held, sems):
    slots, size = held.shape[:2]
    column = lax.axis_index("col")
    share = left_ref.shape[0] // lax.axis_size("col")
    blocks = [
        (flip, offset + start, ref, start)
        for (flip, offset), ref in zip(places, ins)
        for start in range(0, ref.shape[0], size)
    ]

    def copy(j):
        flip, offset = blocks[j][:2]
        start = pl.multiple_of((column ^ flip) * share + offset, 256)
        return pltpu.make_async_copy(left_ref.at[pl.ds(start, size)], held.at[j % slots], sems.at[j % slots])

    def begin():
        for j in range(min(slots, len(blocks))):
            copy(j).start()

    def finish(total):
        for j, (_, _, ref, start) in enumerate(blocks):
            copy(j).wait()
            product = dot0(ref[pl.ds(start, size), :], held[j % slots])
            total = product if total is None else total + product
            if j + slots < len(blocks):
                copy(j + slots).start()
        return total

    return begin, finish


def gram_kernel(places, has_total, left_ref, *refs):
    count = len(places)
    out_ref, held, sems = refs[-3:]
    begin, finish = gram_steps(places, left_ref, refs[:count], held, sems)
    begin()
    out_ref[...] = finish(refs[count][...] if has_total else None)


def gram_of(resident, pieces, places, total=None, earlier=()):
    width = pieces[0].shape[1]
    columns = resident.shape[1]
    slots, block = 4, math.gcd(2048 * 3072, *(piece.shape[0] for piece in pieces))
    height = sum(piece.shape[0] for piece in pieces)
    return pl.pallas_call(
        functools.partial(gram_kernel, places, total is not None),
        in_specs=[HBM] + [VMEM] * (len(pieces) + (total is not None)) + [ANY] * len(earlier),
        out_specs=VMEM,
        out_shape=jax.ShapeDtypeStruct((width, columns), jnp.float32),
        scratch_shapes=[
            pltpu.VMEM((slots, block, columns), jnp.bfloat16),
            pltpu.SemaphoreType.DMA((slots,)),
        ],
        compiler_params=params(16),
        cost_estimate=cost(2 * height * columns * width, 2 * height * (columns + width)),
        name="gram_of",
    )(in_hbm(resident), *pieces, *([] if total is None else [total]), *earlier)


def tiles_kernel(places, rows_ref, *refs):
    ins, (toward_ref, away_ref, table, taken) = refs[:-4], refs[-4:]
    column = lax.axis_index("col")
    share = table.shape[0] // lax.axis_size("col")
    for (flip, offset), ref in zip(places, ins):
        widen(table, (column ^ flip) * share + offset, ref)
    half = taken.shape[0]
    for begins, out_ref in zip(list_starts(2 * half), (toward_ref, away_ref)):
        start = begins + column % 2 * half
        take_rows(lambda i: rows_ref[start + i], table, taken, 0, half)
        out_ref[...] = taken[...].astype(jnp.bfloat16)


def pick_tiles(lists, pieces, places, total):
    width = pieces[0].shape[1]
    half = lists.shape[0] // 4
    return pl.pallas_call(
        functools.partial(tiles_kernel, places),
        in_specs=[SMEM] + [VMEM] * len(pieces),
        out_specs=[VMEM] * 2,
        scratch_shapes=[pltpu.VMEM((total, width), jnp.float32), pltpu.VMEM((half, width), jnp.float32)],
        out_shape=[jax.ShapeDtypeStruct((half, width), jnp.bfloat16)] * 2,
        compiler_params=params(20),
        cost_estimate=cost(0, 4 * total * width),
        name="pick_tiles",
    )(lists, *pieces)


def finish_kernel(first_ref, second_ref, mine_ref, other_ref, total_ref, out_ref):
    half = mine_ref.shape[0] // 2
    core = lax.axis_index("col") % 2
    total = total_ref[...]
    for j, left in enumerate((first_ref, second_ref)):
        for flip, tiles in enumerate((mine_ref, other_ref)):
            rows = left[pl.ds(pl.multiple_of((core ^ flip) * half, half), half), :]
            total = total + dot0(tiles[pl.ds(j * half, half), :], rows)
    out_ref[...] = total.T


def finish(first, second, mine, other, total):
    arrays = (first, second, mine, other, total)
    return pl.pallas_call(
        finish_kernel,
        in_specs=[VMEM] * len(arrays),
        out_specs=VMEM,
        out_shape=jax.ShapeDtypeStruct(total.shape[::-1], jnp.float32),
        compiler_params=params(12),
        cost_estimate=cost(4 * first.size * mine.shape[1], 4 * first.size),
        name="finish",
    )(*arrays)


def shards(panel, stiffness, mass, resident, face_rows, counts):
    slots, nodes, width = panel.shape[1:]
    cols, rows = lax.axis_size("col"), lax.axis_size("row")
    resident = resident[0]
    columns = resident.shape[1]
    weights = mass[0].reshape(slots, 1, nodes)

    def permute(value, move):
        pairs = []
        for source in range(cols * rows):
            target = move(*divmod(source, rows))
            if target is not None:
                pairs.append((source, target[0] * rows + target[1]))
        return lax.ppermute(value, AXES, pairs)

    def across(value):
        return permute(value, lambda c, r: (c ^ 2, r))

    def sibling(value):
        return permute(value, lambda c, r: (c ^ 1, r))

    column, row = lax.axis_index("col"), lax.axis_index("row")
    share = slots * nodes
    per = slots // sum(SPLIT)
    second = per * SPLIT[0]
    offsets = (0, second * nodes)
    lists = face_rows[0].reshape(-1)
    stiffness, panel = stiffness[0], panel[0]
    pieces, far = [], []
    for first, elements in ((0, second), (second, slots - second)):
        pieces.append(apply_chunk(counts, stiffness, panel, weights, first, elements, pieces))
        far.append(across(pieces[-1]))
    first_rows, second_rows, *own = pick_resident(lists, resident, pieces, far[0])
    pieces = own + [sibling(piece) for piece in own]
    places = [(flip, offset) for flip in (0, 1) for offset in (0, share // 2)]
    places[2:2] = [(2, 0)]
    places.append((3, 0))
    total = gram_of(resident, pieces, places)
    last = [far[1], sibling(hold([far[1]], (1,), total)[0])]
    last_places = [(2, offsets[1]), (3, offsets[1])]

    toward, away = pick_tiles(lists, pieces + last, places + last_places, resident.shape[0])
    total = gram_of(resident, last, last_places, total, (toward,))

    def beside(c, r):
        target = r + 1 if r % 2 else r - 1
        return (c, target) if 0 <= target < rows else None

    mine = join(permute(toward, lambda c, r: (c, r ^ 1)), permute(away, beside), total)
    gram = finish(first_rows, second_rows, mine, sibling(mine), total)

    own_rows = columns // rows
    received = lax.all_to_all(gram.reshape(rows, own_rows, width), "row", 0, 0)
    return jnp.sum(received, axis=0)


def solution(mesh):
    in_specs = (
        P("row", "col", None, None),
        P("row", "col", None, None),
        P("row", "col", None),
        P("row", None, "col"),
        P("row", None, None),
        P("row"),
    )
    out_specs = P(("col", "row"), None)
    return jax.shard_map(shards, mesh=mesh, in_specs=in_specs, out_specs=out_specs, check_vma=False)
```

time: 439 us -> 82 us (0.19)
  waiting for transfers between devices: 333 us -> 18.5 us
  other arithmetic: 46.4 us -> 0.63 us
  Pallas kernels: 0 us -> 33 us
  local copies, waits for them, and re-layouts: 20.7 us -> 0.01 us
  blocking collectives: 0 us -> 19.2 us
  matrix products: 17.5 us -> 0 us
  between operations: 14.1 us -> 0.77 us
    psum x1 -> x0, waiting for transfers between devices: 281 us -> none  [shards(): full_gram = lax.psum(partial_gram, 'row')]
    all_gather x1 -> x0, waiting for transfers between devices: 52.9 us -> none  [shards(): whole = lax.all_gather(local_rows, 'col', axis=0, tiled=True)]
    scatter-add x2 -> x0, other arithmetic: 39 us -> none  [the longest x1 19.5 us: shards(): summed = summed.at[prev_rows].add(from_prev.astype(jnp.float32))]
    pallas_call x0 -> x9, Pallas kernels: none -> 33 us  [the longest x1 12.8 us: pick_resident(): pl.pallas_call(functools.partial(pick_kernel, len(pieces)), in_specs=[SME...]
    all_to_all x0 -> x1, blocking collectives: none -> 19.2 us  [shards(): received = lax.all_to_all(gram.reshape(rows, own_rows, width), 'row', 0, 0)]
    ppermute x2 -> x9, waiting for transfers between devices: 0.01 us -> 18.5 us  [permute(): return lax.ppermute(value, AXES, pairs)]
    gather x2 -> x0, local copies, waits for them, and re-layouts: 18.4 us -> none  [the longest x1 9.19 us: shards(): from_prev = passed_along(whole[next_rows], 'row', 1)]
    dot_general x2 -> x0, matrix products: 17.5 us -> none  [the longest x1 10.8 us: shards(): lax.dot_general(columns, summed, contract, preferred_element_type=jnp.flo...]
  transfers between devices with their start and end apart: 4 -> 9, of which waited for: 2 -> 6; matrix products, arithmetic and copies ran while one was open for 8% -> 0% of each run, Pallas kernels for 0% -> 32%
where the time goes in v4:
time: 82 us; the launch traced here: 81.8 us
  Pallas kernels  33 us (40%)
  blocking collectives  19.2 us (23%)
  waiting for transfers between devices  18.5 us (23%)
  starting transfers between devices  9.56 us (12%)
    all_to_all x1, blocking collectives, shards(): received = lax.all_to_all(gram.reshape(rows, own_rows, width), 'row', 0, 0)  19.2 us
    ppermute x9, waiting for transfers between devices, permute(): return lax.ppermute(value, AXES, pairs)  18.5 us
    pallas_call x1, Pallas kernels, pick_resident(): pl.pallas_call(functools.partial(pick_kernel, len(pieces)), in_specs=[SME...  12.8 us
    ppermute x9, starting transfers between devices, permute(): return lax.ppermute(value, AXES, pairs)  9.56 us
    pallas_call x2, Pallas kernels, gram_of(): pl.pallas_call(functools.partial(gram_kernel, places, total is not None),...  8.03 us
    pallas_call x2, Pallas kernels, apply_chunk(): pl.pallas_call(functools.partial(apply_kernel, first), in_specs=[SMEM, HB...  7.33 us
    pallas_call x1, Pallas kernels, pick_tiles(): pl.pallas_call(functools.partial(tiles_kernel, places), in_specs=[SMEM] +...  4.22 us
  transfers between devices with their start and end apart: 9, of which 6 were waited for; matrix products, arithmetic and copies ran while one was open for 0% of the time, Pallas kernels for 32%

profile of v4, /device:TPU:0, one launch (start us, length us, event | category | flops | bytes accessed | tf_op | source)
XLA Modules:
  0.0 81.8 jit_solution(12670167812849777437)
XLA Ops:
  0.7 2.3 %apply.2.refs_4_.refs_0_ = bf16[1536,128]{1,0:T(8,128)(2,1)S(1)} custom-call(s32[1]{0:T(128)S(6)} %copy.8.refs_0_, bf16[12,512,512]{2,1,0:T(8,128)(2,1)} %bitcast.13, bf16[12,512,128]{2,1,0:T(8,128)(2,1)} %bitcast.15, f32[12,1,512]{2,1,0:T(1,128)} %bitcast.17), custom_call_target="tpu_custom_call" | custom-call | flops 201326592 | bytes 2359296 | tf_op jit(solution)/shard_map/apply/pallas_call | solution.py:104
  3.0 0.0 copy-start
  3.0 3.4 %collective-permute-start = (bf16[1536,128]{1,0:T(8,128)(2,1)S(1)}, bf16[1536,128]{1,0:T(8,128)(2,1)S(1)}, u32[]{:S(2)}, u32[]{:S(2)}) collective-permute-start(bf16[1536,128]{1,0:T(8,128)(2,1)S(1)} %apply.2.refs_4_.refs_0_), channel_id=1, source_target_pairs={{0,64},{1,65},{2,66},{3,67},{4,68},{5,69},{6,70},{7,71},{8,72},{9,... | collective-permute-start | bytes 1179656 | tf_op jit(solution)/shard_map/ppermute | solution.py:344
  6.3 5.0 %apply.3.refs_1_ = bf16[4608,128]{1,0:T(8,128)(2,1)S(1)} custom-call(s32[1]{0:T(128)S(6)} %copy.8.refs_0_, bf16[12,512,512]{2,1,0:T(8,128)(2,1)} %bitcast.14, bf16[12,512,128]{2,1,0:T(8,128)(2,1)} %bitcast.16, f32[12,1,512]{2,1,0:T(1,128)} %bitcast.18, bf16[1536,128]{1,0:T(8,128)(2,1)S(1)} %apply.2.refs_4_.refs_0_), custom_call_target="tpu_custom_call" | custom-call | flops 603979776 | bytes 7077888 | tf_op jit(solution)/shard_map/apply/pallas_call | solution.py:104
  11.4 0.3 collective-permute-start.4
  11.7 0.0 copy-done
  11.7 4.2 %collective-permute-done.refs_2_ = bf16[1536,128]{1,0:T(8,128)(2,1)S(1)} collective-permute-done((bf16[1536,128]{1,0:T(8,128)(2,1)S(1)}, bf16[1536,128]{1,0:T(8,128)(2,1)S(1)}, u32[]{:S(2)}, u32[]{:S(2)}) %collective-permute-start) | collective-permute-done | bytes 393248 | tf_op jit(solution)/shard_map/ppermute | solution.py:344
  15.9 12.8 %pick_resident.1 = (bf16[2048,256]{1,0:T(8,128)(2,1)S(1)}, bf16[2048,256]{1,0:T(8,128)(2,1)S(1)}, bf16[3072,128]{1,0:T(8,128)(2,1)S(1)}, bf16[3072,128]{1,0:T(8,128)(2,1)S(1)}, bf16[1536,128]{1,0:T(8,128)(2,1)S(1)}) custom-call(s32[4096]{0:T(1024)S(1)} %bitcast.8, bf16[24576,256]{1,0:T(8,128)(2,1)} %bitcast.10, bf16[1536,128]{1,0:T(8,128)(2,1)S(1)} %apply.2.refs_4_.refs_0_, ...), custom_call_target="tpu_custom_call" | custom-call | bytes 25165824 | tf_op jit(solution)/shard_map/pick_resident/pallas_call | solution.py:159
  28.7 0.1 collective-permute-start.1
  28.8 0.5 collective-permute-start.2
  29.3 0.1 collective-permute-start.3
  29.4 3.4 %collective-permute-done.3.refs_5_ = bf16[1536,128]{1,0:T(8,128)(2,1)S(1)} collective-permute-done((bf16[1536,128]{1,0:T(8,128)(2,1)S(1)}, bf16[1536,128]{1,0:T(8,128)(2,1)S(1)}, u32[]{:S(2)}, u32[]{:S(2)}) %collective-permute-start.3) | collective-permute-done | bytes 393248 | tf_op jit(solution)/shard_map/ppermute | solution.py:344
  32.7 0.0 collective-permute-done.1.refs_3_
  32.7 0.0 collective-permute-done.2.refs_4_
  32.7 4.8 %gram_of.2.refs_1_.refs_2_ = f32[128,256]{1,0:T(8,128)S(1)} custom-call(bf16[24576,256]{1,0:T(8,128)(2,1)} %bitcast.11, bf16[3072,128]{1,0:T(8,128)(2,1)S(1)} %get-tuple-element.14.refs_0_, bf16[3072,128]{1,0:T(8,128)(2,1)S(1)} %get-tuple-element.15.refs_1_, bf16[1536,128]{1,0:T(8,128)(2,1)S(1)} %get-tuple-element.16.refs_2_, ...), custom_call_target="tpu_custom_call" | custom-call | flops 1006632960 | bytes 11796480 | tf_op jit(solution)/shard_map/gram_of/pallas_call | solution.py:264
  37.5 3.2 %collective-permute-done.4.refs_0_.refs_6_ = bf16[4608,128]{1,0:T(8,128)(2,1)S(1)} collective-permute-done((bf16[4608,128]{1,0:T(8,128)(2,1)S(1)}, bf16[4608,128]{1,0:T(8,128)(2,1)S(1)}, u32[]{:S(2)}, u32[]{:S(2)}) %collective-permute-start.4) | collective-permute-done | bytes 1179680 | tf_op jit(solution)/shard_map/ppermute | solution.py:344
  40.7 0.1 hold.1
  40.8 0.1 collective-permute-start.5
  40.9 2.8 %collective-permute-done.5.refs_7_.refs_1_ = bf16[4608,128]{1,0:T(8,128)(2,1)S(1)} collective-permute-done((bf16[4608,128]{1,0:T(8,128)(2,1)S(1)}, bf16[4608,128]{1,0:T(8,128)(2,1)S(1)}, u32[]{:S(2)}, u32[]{:S(2)}) %collective-permute-start.5) | collective-permute-done | bytes 1179680 | tf_op jit(solution)/shard_map/ppermute | solution.py:344
  43.7 4.2 %pick_tiles.1 = (bf16[1024,128]{1,0:T(8,128)(2,1)S(1)}, bf16[1024,128]{1,0:T(8,128)(2,1)S(1)}) custom-call(s32[4096]{0:T(1024)S(1)} %bitcast.9, bf16[3072,128]{1,0:T(8,128)(2,1)S(1)} %get-tuple-element.14.refs_0_, bf16[3072,128]{1,0:T(8,128)(2,1)S(1)} %get-tuple-element.15.refs_1_, bf16[1536,128]{1,0:T(8,128)(2,1)S(1)} %get-tuple-element.16.refs_2_, ...), custom_call_target="tpu_custom_call" | custom-call | bytes 12582912 | tf_op jit(solution)/shard_map/pick_tiles/pallas_call | solution.py:295
  48.0 0.7 collective-permute-start.7
  48.7 4.3 %collective-permute-start.6 = (bf16[1024,128]{1,0:T(8,128)(2,1)S(1)}, bf16[1024,128]{1,0:T(8,128)(2,1)S(1)}, u32[]{:S(2)}, u32[]{:S(2)}) collective-permute-start(bf16[1024,128]{1,0:T(8,128)(2,1)S(1)} %get-tuple-element.17.refs_3_), channel_id=1, source_target_pairs={{0,1},{1,0},{2,3},{3,2},{4,5},{5,4},{6,7},{7,6},{8,9},{9,8},{10,11... | collective-permute-start | bytes 786440 | tf_op jit(solution)/shard_map/ppermute | solution.py:344
  53.0 3.3 %gram_of.3._.total_ref = f32[128,256]{1,0:T(8,128)S(1)} custom-call(bf16[24576,256]{1,0:T(8,128)(2,1)} %bitcast.12, bf16[4608,128]{1,0:T(8,128)(2,1)S(1)} %collective-permute-done.4.refs_0_.refs_6_, bf16[4608,128]{1,0:T(8,128)(2,1)S(1)} %collective-permute-done.5.refs_7_.refs_1_, f32[128,256]{1,0:T(8,128)S(1)} %gram_of.2.refs_1_.refs_2_, ...), custom_call_target="tpu_custom_call" | custom-call | flops 603979776 | bytes 7077888 | tf_op jit(solution)/shard_map/gram_of/pallas_call | solution.py:264
  56.3 0.0 collective-permute-done.7.second_ref
  56.3 3.1 %collective-permute-done.6.first_ref = bf16[1024,128]{1,0:T(8,128)(2,1)S(1)} collective-permute-done((bf16[1024,128]{1,0:T(8,128)(2,1)S(1)}, bf16[1024,128]{1,0:T(8,128)(2,1)S(1)}, u32[]{:S(2)}, u32[]{:S(2)}) %collective-permute-start.6) | collective-permute-done | bytes 262176 | tf_op jit(solution)/shard_map/ppermute | solution.py:344
  59.4 0.1 collective-permute-start.8
  59.5 1.9 %collective-permute-done.8.other_ref = bf16[2048,128]{1,0:T(8,128)(2,1)S(1)} collective-permute-done((bf16[2048,128]{1,0:T(8,128)(2,1)S(1)}, bf16[2048,128]{1,0:T(8,128)(2,1)S(1)}, u32[]{:S(2)}, u32[]{:S(2)}) %collective-permute-start.8) | collective-permute-done | bytes 524320 | tf_op jit(solution)/shard_map/ppermute | solution.py:344
  61.4 0.5 finish.1
  61.9 19.2 %all_to_all.5 = f32[32,8,128]{2,1,0:T(8,128)S(1)} all-to-all(f32[32,8,128]{2,1,0:T(8,128)S(1)} %bitcast.7), channel_id=1, replica_groups=mesh['col'=4,'row'=32] {'row'}, dimensions={0} | all-to-all | bytes 262144 | tf_op jit(solution)/shard_map/all_to_all | solution.py:383
  81.1 0.6 reduce_sum.9
  (2 shorter events, 0.0 us)
Async XLA Ops:
  3.0 8.7 %copy-start = (s32[1,2,2048]{2,1,0:T(2,128)S(1)}, s32[1,2,2048]{2,1,0:T(2,128)}, u32[]{:S(2)}) copy-start(s32[1,2,2048]{2,1,0:T(2,128)} %param.10) | copy-start | bytes 49156
  3.0 12.9 %collective-permute-start = (bf16[1536,128]{1,0:T(8,128)(2,1)S(1)}, bf16[1536,128]{1,0:T(8,128)(2,1)S(1)}, u32[]{:S(2)}, u32[]{:S(2)}) collective-permute-start(bf16[1536,128]{1,0:T(8,128)(2,1)S(1)} %apply.2.refs_4_.refs_0_), channel_id=1, source_target_pairs={{0,64},{1,65},{2,66},{3,67},{4,68},{5,69},{6,70},{7,71},{8,72},{9,... | collective-permute-start | bytes 1179656 | tf_op jit(solution)/shard_map/ppermute | solution.py:344
  11.4 29.4 %collective-permute-start.4 = (bf16[4608,128]{1,0:T(8,128)(2,1)S(1)}, bf16[4608,128]{1,0:T(8,128)(2,1)S(1)}, u32[]{:S(2)}, u32[]{:S(2)}) collective-permute-start(bf16[4608,128]{1,0:T(8,128)(2,1)S(1)} %apply.3.refs_1_), channel_id=1, source_target_pairs={{0,64},{1,65},{2,66},{3,67},{4,68},{5,69},{6,70},{7,71},{8,72},{9,... | collective-permute-start | bytes 3538952 | tf_op jit(solution)/shard_map/ppermute | solution.py:344
  28.7 4.1 %collective-permute-start.1 = (bf16[3072,128]{1,0:T(8,128)(2,1)S(1)}, bf16[3072,128]{1,0:T(8,128)(2,1)S(1)}, u32[]{:S(2)}, u32[]{:S(2)}) collective-permute-start(bf16[3072,128]{1,0:T(8,128)(2,1)S(1)} %get-tuple-element.14.refs_0_), channel_id=1, source_target_pairs={{0,32},{1,33},{2,34},{3,35},{4,36},{5,37},{6,38},{7,39},{8,40},{9,... | collective-permute-start | bytes 2359304 | tf_op jit(solution)/shard_map/ppermute | solution.py:344
  28.8 4.0 %collective-permute-start.2 = (bf16[3072,128]{1,0:T(8,128)(2,1)S(1)}, bf16[3072,128]{1,0:T(8,128)(2,1)S(1)}, u32[]{:S(2)}, u32[]{:S(2)}) collective-permute-start(bf16[3072,128]{1,0:T(8,128)(2,1)S(1)} %get-tuple-element.15.refs_1_), channel_id=1, source_target_pairs={{0,32},{1,33},{2,34},{3,35},{4,36},{5,37},{6,38},{7,39},{8,40},{9,... | collective-permute-start | bytes 2359304 | tf_op jit(solution)/shard_map/ppermute | solution.py:344
  29.3 3.5 %collective-permute-start.3 = (bf16[1536,128]{1,0:T(8,128)(2,1)S(1)}, bf16[1536,128]{1,0:T(8,128)(2,1)S(1)}, u32[]{:S(2)}, u32[]{:S(2)}) collective-permute-start(bf16[1536,128]{1,0:T(8,128)(2,1)S(1)} %get-tuple-element.16.refs_2_), channel_id=1, source_target_pairs={{0,32},{1,33},{2,34},{3,35},{4,36},{5,37},{6,38},{7,39},{8,40},{9,... | collective-permute-start | bytes 1179656 | tf_op jit(solution)/shard_map/ppermute | solution.py:344
  40.8 2.9 %collective-permute-start.5 = (bf16[4608,128]{1,0:T(8,128)(2,1)S(1)}, bf16[4608,128]{1,0:T(8,128)(2,1)S(1)}, u32[]{:S(2)}, u32[]{:S(2)}) collective-permute-start(bf16[4608,128]{1,0:T(8,128)(2,1)S(1)} %hold.1), channel_id=1, source_target_pairs={{0,32},{1,33},{2,34},{3,35},{4,36},{5,37},{6,38},{7,39},{8,40},{9,... | collective-permute-start | bytes 3538952 | tf_op jit(solution)/shard_map/ppermute | solution.py:344
  48.0 8.3 %collective-permute-start.7 = (bf16[1024,128]{1,0:T(8,128)(2,1)S(1)}, bf16[1024,128]{1,0:T(8,128)(2,1)S(1)}, u32[]{:S(2)}, u32[]{:S(2)}) collective-permute-start(bf16[1024,128]{1,0:T(8,128)(2,1)S(1)} %get-tuple-element.18), channel_id=1, source_target_pairs={{1,2},{2,1},{3,4},{4,3},{5,6},{6,5},{7,8},{8,7},{9,10},{10,9},{11,... | collective-permute-start | bytes 786440 | tf_op jit(solution)/shard_map/ppermute | solution.py:344
  48.7 10.7 %collective-permute-start.6 = (bf16[1024,128]{1,0:T(8,128)(2,1)S(1)}, bf16[1024,128]{1,0:T(8,128)(2,1)S(1)}, u32[]{:S(2)}, u32[]{:S(2)}) collective-permute-start(bf16[1024,128]{1,0:T(8,128)(2,1)S(1)} %get-tuple-element.17.refs_3_), channel_id=1, source_target_pairs={{0,1},{1,0},{2,3},{3,2},{4,5},{5,4},{6,7},{7,6},{8,9},{9,8},{10,11... | collective-permute-start | bytes 786440 | tf_op jit(solution)/shard_map/ppermute | solution.py:344
  59.4 2.0 %collective-permute-start.8 = (bf16[2048,128]{1,0:T(8,128)(2,1)S(1)}, bf16[2048,128]{1,0:T(8,128)(2,1)S(1)}, u32[]{:S(2)}, u32[]{:S(2)}) collective-permute-start(bf16[2048,128]{1,0:T(8,128)(2,1)S(1)} %join.1.mine_ref), channel_id=1, source_target_pairs={{0,32},{1,33},{2,34},{3,35},{4,36},{5,37},{6,38},{7,39},{8,40},{9,... | collective-permute-start | bytes 1572872 | tf_op jit(solution)/shard_map/ppermute | solution.py:344

commit v5 on v4

--- a/solution.py
+++ b/solution.py
@@ -198,23 +198,25 @@
     )(*values, *earlier)
 
 
-def join_kernel(first_ref, second_ref, _, out_ref):
-    size = first_ref.shape[0]
-    out_ref[pl.ds(0, size), :] = first_ref[...]
-    out_ref[pl.ds(size, size), :] = second_ref[...]
-
-
-def join(first, second, earlier):
-    shape = (2 * first.shape[0], first.shape[1])
+def join_kernel(*refs):
+    start = 0
+    for part in refs[:-2]:
+        size = part.shape[0]
+        refs[-1][pl.ds(start, size), :] = part[...]
+        start += size
+
+
+def join(parts, earlier):
+    shape = (sum(part.shape[0] for part in parts), parts[0].shape[1])
     return pl.pallas_call(
         join_kernel,
-        in_specs=[VMEM, VMEM, ANY],
+        in_specs=[VMEM] * len(parts) + [ANY],
         out_specs=VMEM,
-        out_shape=jax.ShapeDtypeStruct(shape, first.dtype),
+        out_shape=jax.ShapeDtypeStruct(shape, parts[0].dtype),
         compiler_params=params(8),
-        cost_estimate=cost(0, 8 * first.size),
+        cost_estimate=cost(0, 4 * shape[0] * shape[1]),
         name="join",
-    )(first, second, earlier)
+    )(*parts, earlier)
 
 
 def gram_steps(places, left_ref, ins, held, sems):
@@ -276,32 +278,41 @@
     )(in_hbm(resident), *pieces, *([] if total is None else [total]), *earlier)
 
 
-def tiles_kernel(places, rows_ref, *refs):
-    ins, (toward_ref, away_ref, table, taken) = refs[:-4], refs[-4:]
+def tiles_kernel(places, away, rows_ref, *refs):
+    count = len(places)
+    ins, outs, (table, taken) = refs[:count], refs[count + 1 - away : -2], refs[-2:]
     column = lax.axis_index("col")
     share = table.shape[0] // lax.axis_size("col")
     for (flip, offset), ref in zip(places, ins):
         widen(table, (column ^ flip) * share + offset, ref)
     half = taken.shape[0]
-    for begins, out_ref in zip(list_starts(2 * half), (toward_ref, away_ref)):
-        start = begins + column % 2 * half
-        take_rows(lambda i: rows_ref[start + i], table, taken, 0, half)
-        out_ref[...] = taken[...].astype(jnp.bfloat16)
-
-
-def pick_tiles(lists, pieces, places, total):
+    start = list_starts(2 * half)[away] + column % 2 * half
+    take_rows(lambda i: rows_ref[start + i], table, taken, 0, half)
+    size = outs[0].shape[0]
+    for j, out_ref in enumerate(outs):
+        out_ref[...] = taken[pl.ds(j * size, size), :].astype(jnp.bfloat16)
+    if away:
+        row, rows = lax.axis_index("row"), lax.axis_size("row")
+
+        @pl.when((row == 0) | (row == rows - 1))
+        def _():
+            for out_ref in outs:
+                out_ref[...] = jnp.zeros(out_ref.shape, out_ref.dtype)
+
+
+def pick_tiles(lists, pieces, places, total, away, parts, *earlier):
     width = pieces[0].shape[1]
     half = lists.shape[0] // 4
     return pl.pallas_call(
-        functools.partial(tiles_kernel, places),
-        in_specs=[SMEM] + [VMEM] * len(pieces),
-        out_specs=[VMEM] * 2,
+        functools.partial(tiles_kernel, places, away),
+        in_specs=[SMEM] + [VMEM] * len(pieces) + [ANY] * len(earlier),
+        out_specs=[VMEM] * parts,
         scratch_shapes=[pltpu.VMEM((total, width), jnp.float32), pltpu.VMEM((half, width), jnp.float32)],
-        out_shape=[jax.ShapeDtypeStruct((half, width), jnp.bfloat16)] * 2,
+        out_shape=[jax.ShapeDtypeStruct((half // parts, width), jnp.bfloat16)] * parts,
         compiler_params=params(20),
         cost_estimate=cost(0, 4 * total * width),
         name="pick_tiles",
-    )(lists, *pieces)
+    )(lists, *pieces, *earlier)
 
 
 def finish_kernel(first_ref, second_ref, mine_ref, other_ref, total_ref, out_ref):
@@ -338,9 +349,8 @@
     def permute(value, move):
         pairs = []
         for source in range(cols * rows):
-            target = move(*divmod(source, rows))
-            if target is not None:
-                pairs.append((source, target[0] * rows + target[1]))
+            column, row = move(*divmod(source, rows))
+            pairs.append((source, column * rows + row))
         return lax.ppermute(value, AXES, pairs)
 
     def across(value):
@@ -369,14 +379,16 @@
     last = [far[1], sibling(hold([far[1]], (1,), total)[0])]
     last_places = [(2, offsets[1]), (3, offsets[1])]
 
-    toward, away = pick_tiles(lists, pieces + last, places + last_places, resident.shape[0])
-    total = gram_of(resident, last, last_places, total, (toward,))
+    rest = (lists, pieces + last, places + last_places, resident.shape[0])
+    (away,) = pick_tiles(*rest, 1, 1)
+    toward = pick_tiles(*rest, 0, 2, away)
+    total = gram_of(resident, last, last_places, total, (toward[0],))
 
     def beside(c, r):
-        target = r + 1 if r % 2 else r - 1
-        return (c, target) if 0 <= target < rows else None
-
-    mine = join(permute(toward, lambda c, r: (c, r ^ 1)), permute(away, beside), total)
+        return c, (r + 1 if r % 2 else r - 1) % rows
+
+    met = [permute(part, lambda c, r: (c, r ^ 1)) for part in toward] + [permute(away, beside)]
+    mine = join(met, total)
     gram = finish(first_rows, second_rows, mine, sibling(mine), total)
 
     own_rows = columns // rows

time: 82 us -> 80.3 us (0.979)
  blocking collectives: 19.2 us -> 11.7 us
  starting transfers between devices: 9.56 us -> 14 us
  Pallas kernels: 33 us -> 34.7 us
    all_to_all x1, blocking collectives: 19.2 us -> 11.7 us  [shards(): received = lax.all_to_all(gram.reshape(rows, own_rows, width), 'row', 0, 0)]
    ppermute x9 -> x10, starting transfers between devices: 9.56 us -> 14 us  [permute(): return lax.ppermute(value, AXES, pairs)]
    pallas_call x2 -> x3, Pallas kernels: 4.25 us -> 5.91 us  [the longest x2 5.87 us: pick_tiles(): pl.pallas_call(functools.partial(tiles_kernel, places, away), in_specs=[S...]
    ppermute x9 -> x10, waiting for transfers between devices: 18.5 us -> 18.3 us  [permute(): return lax.ppermute(value, AXES, pairs)]
  transfers between devices with their start and end apart: 9 -> 10, of which waited for: 6 -> 7; matrix products, arithmetic and copies ran while one was open for 0% -> 0% of each run, Pallas kernels for 32% -> 36%
where the time goes in v5:
time: 80.3 us; the launch traced here: 80.1 us
  Pallas kernels  34.7 us (43%)
  waiting for transfers between devices  18.3 us (23%)
  starting transfers between devices  14 us (17%)
  blocking collectives  11.7 us (15%)
    ppermute x10, waiting for transfers between devices, permute(): return lax.ppermute(value, AXES, pairs)  18.3 us
    ppermute x10, starting transfers between devices, permute(): return lax.ppermute(value, AXES, pairs)  14 us
    pallas_call x1, Pallas kernels, pick_resident(): pl.pallas_call(functools.partial(pick_kernel, len(pieces)), in_specs=[SME...  12.8 us
    all_to_all x1, blocking collectives, shards(): received = lax.all_to_all(gram.reshape(rows, own_rows, width), 'row', 0, 0)  11.7 us
    pallas_call x2, Pallas kernels, gram_of(): pl.pallas_call(functools.partial(gram_kernel, places, total is not None),...  8.03 us
    pallas_call x2, Pallas kernels, apply_chunk(): pl.pallas_call(functools.partial(apply_kernel, first), in_specs=[SMEM, HB...  7.33 us
    pallas_call x2, Pallas kernels, pick_tiles(): pl.pallas_call(functools.partial(tiles_kernel, places, away), in_specs=[S...  5.87 us
  transfers between devices with their start and end apart: 10, of which 7 were waited for; matrix products, arithmetic and copies ran while one was open for 0% of the time, Pallas kernels for 36%

profile of v5, /device:TPU:0, one launch (start us, length us, event | category | flops | bytes accessed | tf_op | source)
XLA Modules:
  0.0 80.1 jit_solution(3692719084361655498)
XLA Ops:
  0.7 2.3 %apply.2.refs_4_.refs_0_ = bf16[1536,128]{1,0:T(8,128)(2,1)S(1)} custom-call(s32[1]{0:T(128)S(6)} %copy.8.refs_0_, bf16[12,512,512]{2,1,0:T(8,128)(2,1)} %bitcast.14, bf16[12,512,128]{2,1,0:T(8,128)(2,1)} %bitcast.16, f32[12,1,512]{2,1,0:T(1,128)} %bitcast.18), custom_call_target="tpu_custom_call" | custom-call | flops 201326592 | bytes 2359296 | tf_op jit(solution)/shard_map/apply/pallas_call | solution.py:104
  3.0 0.0 copy-start
  3.0 3.4 %collective-permute-start = (bf16[1536,128]{1,0:T(8,128)(2,1)S(1)}, bf16[1536,128]{1,0:T(8,128)(2,1)S(1)}, u32[]{:S(2)}, u32[]{:S(2)}) collective-permute-start(bf16[1536,128]{1,0:T(8,128)(2,1)S(1)} %apply.2.refs_4_.refs_0_), channel_id=1, source_target_pairs={{0,64},{1,65},{2,66},{3,67},{4,68},{5,69},{6,70},{7,71},{8,72},{9,... | collective-permute-start | bytes 1179656 | tf_op jit(solution)/shard_map/ppermute | solution.py:354
  6.3 5.0 %apply.3.refs_1_ = bf16[4608,128]{1,0:T(8,128)(2,1)S(1)} custom-call(s32[1]{0:T(128)S(6)} %copy.8.refs_0_, bf16[12,512,512]{2,1,0:T(8,128)(2,1)} %bitcast.15, bf16[12,512,128]{2,1,0:T(8,128)(2,1)} %bitcast.17, f32[12,1,512]{2,1,0:T(1,128)} %bitcast.19, bf16[1536,128]{1,0:T(8,128)(2,1)S(1)} %apply.2.refs_4_.refs_0_), custom_call_target="tpu_custom_call" | custom-call | flops 603979776 | bytes 7077888 | tf_op jit(solution)/shard_map/apply/pallas_call | solution.py:104
  11.4 0.3 collective-permute-start.4
  11.7 0.0 copy-done
  11.7 4.2 %collective-permute-done.refs_2_ = bf16[1536,128]{1,0:T(8,128)(2,1)S(1)} collective-permute-done((bf16[1536,128]{1,0:T(8,128)(2,1)S(1)}, bf16[1536,128]{1,0:T(8,128)(2,1)S(1)}, u32[]{:S(2)}, u32[]{:S(2)}) %collective-permute-start) | collective-permute-done | bytes 393248 | tf_op jit(solution)/shard_map/ppermute | solution.py:354
  15.9 12.8 %pick_resident.1 = (bf16[2048,256]{1,0:T(8,128)(2,1)S(1)}, bf16[2048,256]{1,0:T(8,128)(2,1)S(1)}, bf16[3072,128]{1,0:T(8,128)(2,1)S(1)}, bf16[3072,128]{1,0:T(8,128)(2,1)S(1)}, bf16[1536,128]{1,0:T(8,128)(2,1)S(1)}) custom-call(s32[4096]{0:T(1024)S(1)} %bitcast.8, bf16[24576,256]{1,0:T(8,128)(2,1)} %bitcast.11, bf16[1536,128]{1,0:T(8,128)(2,1)S(1)} %apply.2.refs_4_.refs_0_, ...), custom_call_target="tpu_custom_call" | custom-call | bytes 25165824 | tf_op jit(solution)/shard_map/pick_resident/pallas_call | solution.py:159
  28.7 0.1 collective-permute-start.1
  28.8 0.5 collective-permute-start.2
  29.3 0.1 collective-permute-start.3
  29.4 3.4 %collective-permute-done.3.refs_5_ = bf16[1536,128]{1,0:T(8,128)(2,1)S(1)} collective-permute-done((bf16[1536,128]{1,0:T(8,128)(2,1)S(1)}, bf16[1536,128]{1,0:T(8,128)(2,1)S(1)}, u32[]{:S(2)}, u32[]{:S(2)}) %collective-permute-start.3) | collective-permute-done | bytes 393248 | tf_op jit(solution)/shard_map/ppermute | solution.py:354
  32.7 0.0 collective-permute-done.1.refs_3_
  32.7 0.0 collective-permute-done.2.refs_4_
  32.7 4.8 %gram_of.2.refs_1_.refs_2_ = f32[128,256]{1,0:T(8,128)S(1)} custom-call(bf16[24576,256]{1,0:T(8,128)(2,1)} %bitcast.12, bf16[3072,128]{1,0:T(8,128)(2,1)S(1)} %get-tuple-element.14.refs_0_, bf16[3072,128]{1,0:T(8,128)(2,1)S(1)} %get-tuple-element.15.refs_1_, bf16[1536,128]{1,0:T(8,128)(2,1)S(1)} %get-tuple-element.16.refs_2_, ...), custom_call_target="tpu_custom_call" | custom-call | flops 1006632960 | bytes 11796480 | tf_op jit(solution)/shard_map/gram_of/pallas_call | solution.py:266
  37.5 3.2 %collective-permute-done.4.refs_0_.refs_6_ = bf16[4608,128]{1,0:T(8,128)(2,1)S(1)} collective-permute-done((bf16[4608,128]{1,0:T(8,128)(2,1)S(1)}, bf16[4608,128]{1,0:T(8,128)(2,1)S(1)}, u32[]{:S(2)}, u32[]{:S(2)}) %collective-permute-start.4) | collective-permute-done | bytes 1179680 | tf_op jit(solution)/shard_map/ppermute | solution.py:354
  40.7 0.1 hold.1
  40.8 0.1 collective-permute-start.5
  40.9 2.8 %collective-permute-done.5.refs_7_.refs_1_ = bf16[4608,128]{1,0:T(8,128)(2,1)S(1)} collective-permute-done((bf16[4608,128]{1,0:T(8,128)(2,1)S(1)}, bf16[4608,128]{1,0:T(8,128)(2,1)S(1)}, u32[]{:S(2)}, u32[]{:S(2)}) %collective-permute-start.5) | collective-permute-done | bytes 1179680 | tf_op jit(solution)/shard_map/ppermute | solution.py:354
  43.7 3.0 %pick_tiles.2.refs_8_ = bf16[1024,128]{1,0:T(8,128)(2,1)S(1)} custom-call(s32[4096]{0:T(1024)S(1)} %bitcast.9, bf16[3072,128]{1,0:T(8,128)(2,1)S(1)} %get-tuple-element.14.refs_0_, bf16[3072,128]{1,0:T(8,128)(2,1)S(1)} %get-tuple-element.15.refs_1_, bf16[1536,128]{1,0:T(8,128)(2,1)S(1)} %get-tuple-element.16.refs_2_, ...), custom_call_target="tpu_custom_call" | custom-call | bytes 12582912 | tf_op jit(solution)/shard_map/pick_tiles/pallas_call | solution.py:306
  46.7 7.4 %collective-permute-start.8 = (bf16[1024,128]{1,0:T(8,128)(2,1)S(1)}, bf16[1024,128]{1,0:T(8,128)(2,1)S(1)}, u32[]{:S(2)}, u32[]{:S(2)}) collective-permute-start(bf16[1024,128]{1,0:T(8,128)(2,1)S(1)} %pick_tiles.2.refs_8_), channel_id=1, source_target_pairs={{0,31},{1,2},{2,1},{3,4},{4,3},{5,6},{6,5},{7,8},{8,7},{9,10},{10,... | collective-permute-start | bytes 786440 | tf_op jit(solution)/shard_map/ppermute | solution.py:354
  54.1 2.9 %pick_tiles.3 = (bf16[512,128]{1,0:T(8,128)(2,1)S(1)}, bf16[512,128]{1,0:T(8,128)(2,1)S(1)}) custom-call(s32[4096]{0:T(1024)S(1)} %bitcast.10, bf16[3072,128]{1,0:T(8,128)(2,1)S(1)} %get-tuple-element.14.refs_0_, bf16[3072,128]{1,0:T(8,128)(2,1)S(1)} %get-tuple-element.15.refs_1_, bf16[1536,128]{1,0:T(8,128)(2,1)S(1)} %get-tuple-element.16.refs_2_, ...), custom_call_target="tpu_custom_call" | custom-call | bytes 12582912 | tf_op jit(solution)/shard_map/pick_tiles/pallas_call | solution.py:306
  57.0 0.1 collective-permute-start.7
  57.1 2.0 %collective-permute-start.6 = (bf16[512,128]{1,0:T(8,128)(2,1)S(1)}, bf16[512,128]{1,0:T(8,128)(2,1)S(1)}, u32[]{:S(2)}, u32[]{:S(2)}) collective-permute-start(bf16[512,128]{1,0:T(8,128)(2,1)S(1)} %get-tuple-element.17.refs_3_), channel_id=1, source_target_pairs={{0,1},{1,0},{2,3},{3,2},{4,5},{5,4},{6,7},{7,6},{8,9},{9,8},{10,11... | collective-permute-start | bytes 393224 | tf_op jit(solution)/shard_map/ppermute | solution.py:354
  59.1 3.3 %gram_of.3.refs_3_.total_ref = f32[128,256]{1,0:T(8,128)S(1)} custom-call(bf16[24576,256]{1,0:T(8,128)(2,1)} %bitcast.13, bf16[4608,128]{1,0:T(8,128)(2,1)S(1)} %collective-permute-done.4.refs_0_.refs_6_, bf16[4608,128]{1,0:T(8,128)(2,1)S(1)} %collective-permute-done.5.refs_7_.refs_1_, f32[128,256]{1,0:T(8,128)S(1)} %gram_of.2.refs_1_.refs_2_, ...), custom_call_target="tpu_custom_call" | custom-call | flops 603979776 | bytes 7077888 | tf_op jit(solution)/shard_map/gram_of/pallas_call | solution.py:266
  62.4 1.1 %collective-permute-done.7.refs_1_ = bf16[512,128]{1,0:T(8,128)(2,1)S(1)} collective-permute-done((bf16[512,128]{1,0:T(8,128)(2,1)S(1)}, bf16[512,128]{1,0:T(8,128)(2,1)S(1)}, u32[]{:S(2)}, u32[]{:S(2)}) %collective-permute-start.7) | collective-permute-done | bytes 131104 | tf_op jit(solution)/shard_map/ppermute | solution.py:354
  63.5 1.7 %collective-permute-done.6.refs_0_ = bf16[512,128]{1,0:T(8,128)(2,1)S(1)} collective-permute-done((bf16[512,128]{1,0:T(8,128)(2,1)S(1)}, bf16[512,128]{1,0:T(8,128)(2,1)S(1)}, u32[]{:S(2)}, u32[]{:S(2)}) %collective-permute-start.6) | collective-permute-done | bytes 131104 | tf_op jit(solution)/shard_map/ppermute | solution.py:354
  65.2 0.0 collective-permute-done.8.refs_2_
  65.2 0.1 collective-permute-start.9
  65.3 1.9 %collective-permute-done.9.other_ref = bf16[2048,128]{1,0:T(8,128)(2,1)S(1)} collective-permute-done((bf16[2048,128]{1,0:T(8,128)(2,1)S(1)}, bf16[2048,128]{1,0:T(8,128)(2,1)S(1)}, u32[]{:S(2)}, u32[]{:S(2)}) %collective-permute-start.9) | collective-permute-done | bytes 524320 | tf_op jit(solution)/shard_map/ppermute | solution.py:354
  67.2 0.5 finish.1
  67.7 11.7 %all_to_all.5 = f32[32,8,128]{2,1,0:T(8,128)S(1)} all-to-all(f32[32,8,128]{2,1,0:T(8,128)S(1)} %bitcast.7), channel_id=1, replica_groups=mesh['col'=4,'row'=32] {'row'}, dimensions={0} | all-to-all | bytes 262144 | tf_op jit(solution)/shard_map/all_to_all | solution.py:395
  79.5 0.6 reduce_sum.9
  (2 shorter events, 0.0 us)
Async XLA Ops:
  3.0 8.7 %copy-start = (s32[1,2,2048]{2,1,0:T(2,128)S(1)}, s32[1,2,2048]{2,1,0:T(2,128)}, u32[]{:S(2)}) copy-start(s32[1,2,2048]{2,1,0:T(2,128)} %param.10) | copy-start | bytes 49156
  3.0 12.9 %collective-permute-start = (bf16[1536,128]{1,0:T(8,128)(2,1)S(1)}, bf16[1536,128]{1,0:T(8,128)(2,1)S(1)}, u32[]{:S(2)}, u32[]{:S(2)}) collective-permute-start(bf16[1536,128]{1,0:T(8,128)(2,1)S(1)} %apply.2.refs_4_.refs_0_), channel_id=1, source_target_pairs={{0,64},{1,65},{2,66},{3,67},{4,68},{5,69},{6,70},{7,71},{8,72},{9,... | collective-permute-start | bytes 1179656 | tf_op jit(solution)/shard_map/ppermute | solution.py:354
  11.4 29.4 %collective-permute-start.4 = (bf16[4608,128]{1,0:T(8,128)(2,1)S(1)}, bf16[4608,128]{1,0:T(8,128)(2,1)S(1)}, u32[]{:S(2)}, u32[]{:S(2)}) collective-permute-start(bf16[4608,128]{1,0:T(8,128)(2,1)S(1)} %apply.3.refs_1_), channel_id=1, source_target_pairs={{0,64},{1,65},{2,66},{3,67},{4,68},{5,69},{6,70},{7,71},{8,72},{9,... | collective-permute-start | bytes 3538952 | tf_op jit(solution)/shard_map/ppermute | solution.py:354
  28.7 4.1 %collective-permute-start.1 = (bf16[3072,128]{1,0:T(8,128)(2,1)S(1)}, bf16[3072,128]{1,0:T(8,128)(2,1)S(1)}, u32[]{:S(2)}, u32[]{:S(2)}) collective-permute-start(bf16[3072,128]{1,0:T(8,128)(2,1)S(1)} %get-tuple-element.14.refs_0_), channel_id=1, source_target_pairs={{0,32},{1,33},{2,34},{3,35},{4,36},{5,37},{6,38},{7,39},{8,40},{9,... | collective-permute-start | bytes 2359304 | tf_op jit(solution)/shard_map/ppermute | solution.py:354
  28.8 4.0 %collective-permute-start.2 = (bf16[3072,128]{1,0:T(8,128)(2,1)S(1)}, bf16[3072,128]{1,0:T(8,128)(2,1)S(1)}, u32[]{:S(2)}, u32[]{:S(2)}) collective-permute-start(bf16[3072,128]{1,0:T(8,128)(2,1)S(1)} %get-tuple-element.15.refs_1_), channel_id=1, source_target_pairs={{0,32},{1,33},{2,34},{3,35},{4,36},{5,37},{6,38},{7,39},{8,40},{9,... | collective-permute-start | bytes 2359304 | tf_op jit(solution)/shard_map/ppermute | solution.py:354
  29.3 3.5 %collective-permute-start.3 = (bf16[1536,128]{1,0:T(8,128)(2,1)S(1)}, bf16[1536,128]{1,0:T(8,128)(2,1)S(1)}, u32[]{:S(2)}, u32[]{:S(2)}) collective-permute-start(bf16[1536,128]{1,0:T(8,128)(2,1)S(1)} %get-tuple-element.16.refs_2_), channel_id=1, source_target_pairs={{0,32},{1,33},{2,34},{3,35},{4,36},{5,37},{6,38},{7,39},{8,40},{9,... | collective-permute-start | bytes 1179656 | tf_op jit(solution)/shard_map/ppermute | solution.py:354
  40.8 2.9 %collective-permute-start.5 = (bf16[4608,128]{1,0:T(8,128)(2,1)S(1)}, bf16[4608,128]{1,0:T(8,128)(2,1)S(1)}, u32[]{:S(2)}, u32[]{:S(2)}) collective-permute-start(bf16[4608,128]{1,0:T(8,128)(2,1)S(1)} %hold.1), channel_id=1, source_target_pairs={{0,32},{1,33},{2,34},{3,35},{4,36},{5,37},{6,38},{7,39},{8,40},{9,... | collective-permute-start | bytes 3538952 | tf_op jit(solution)/shard_map/ppermute | solution.py:354
  46.7 18.4 %collective-permute-start.8 = (bf16[1024,128]{1,0:T(8,128)(2,1)S(1)}, bf16[1024,128]{1,0:T(8,128)(2,1)S(1)}, u32[]{:S(2)}, u32[]{:S(2)}) collective-permute-start(bf16[1024,128]{1,0:T(8,128)(2,1)S(1)} %pick_tiles.2.refs_8_), channel_id=1, source_target_pairs={{0,31},{1,2},{2,1},{3,4},{4,3},{5,6},{6,5},{7,8},{8,7},{9,10},{10,... | collective-permute-start | bytes 786440 | tf_op jit(solution)/shard_map/ppermute | solution.py:354
  57.0 6.5 %collective-permute-start.7 = (bf16[512,128]{1,0:T(8,128)(2,1)S(1)}, bf16[512,128]{1,0:T(8,128)(2,1)S(1)}, u32[]{:S(2)}, u32[]{:S(2)}) collective-permute-start(bf16[512,128]{1,0:T(8,128)(2,1)S(1)} %get-tuple-element.18), channel_id=1, source_target_pairs={{0,1},{1,0},{2,3},{3,2},{4,5},{5,4},{6,7},{7,6},{8,9},{9,8},{10,11... | collective-permute-start | bytes 393224 | tf_op jit(solution)/shard_map/ppermute | solution.py:354
  57.1 8.1 %collective-permute-start.6 = (bf16[512,128]{1,0:T(8,128)(2,1)S(1)}, bf16[512,128]{1,0:T(8,128)(2,1)S(1)}, u32[]{:S(2)}, u32[]{:S(2)}) collective-permute-start(bf16[512,128]{1,0:T(8,128)(2,1)S(1)} %get-tuple-element.17.refs_3_), channel_id=1, source_target_pairs={{0,1},{1,0},{2,3},{3,2},{4,5},{5,4},{6,7},{7,6},{8,9},{9,8},{10,11... | collective-permute-start | bytes 393224 | tf_op jit(solution)/shard_map/ppermute | solution.py:354
  65.2 2.0 %collective-permute-start.9 = (bf16[2048,128]{1,0:T(8,128)(2,1)S(1)}, bf16[2048,128]{1,0:T(8,128)(2,1)S(1)}, u32[]{:S(2)}, u32[]{:S(2)}) collective-permute-start(bf16[2048,128]{1,0:T(8,128)(2,1)S(1)} %join.1.mine_ref), channel_id=1, source_target_pairs={{0,32},{1,33},{2,34},{3,35},{4,36},{5,37},{6,38},{7,39},{8,40},{9,... | collective-permute-start | bytes 1572872 | tf_op jit(solution)/shard_map/ppermute | solution.py:354
